TPU v7x, 128 devices: a whole 4x4x4 slice. The times are simulated.
128 devices in a mesh: comp: 2 (over y_hi), gx: 16 (over x, z), gy: 4 (over y_lo, core).
Axes of the slice: x: 4, y: 4 (y_hi: 2, y_lo: 2; y = y_hi * 2 + y_lo), z: 4, core: 2. Of those that a mesh axis runs over, the one named last changes fastest.
Arguments:
- state: float32 [2, 16, 2048, 512], P('comp', None, 'gx', 'gy'), may hold values from -6 to 6
- diffusivity: float32 [2, 2048, 512], P('comp', 'gx', 'gy'), may hold values from 0.02 to 0.24
- mixing: float32 [2, 16, 2048, 512], P('comp', None, 'gx', 'gy'), may hold values from 0.1 to 4
- sea_mask: int32 [2048, 512], P('gx', 'gy'), may hold values 0 or 1
- source_row: int32 [2, 2048, 4, 2], P('comp', 'gx', 'gy'), may hold values from 0 to 2047, as said below
- regrid_weight: float32 [2, 2048, 2, 512, 128], P('comp', 'gx', None, 'gy'), may hold values from 0 to 1, as said below
Outputs:
- new_state: float32 [2, 16, 2048, 512], P('comp', None, 'gx', 'gy')
Inputs may be any that keep to these rules, and one draw needn't show every extreme that they name: `source_row`: A source row lies in the other component at the same index along gy as its destination row. With a shift d drawn for each component and each index j along gy: atmosphere row x intersects ocean rows (x // 2 + k + d) mod 2048, ocean row x intersects atmosphere rows (2 x + k + d) mod 2048, for k < 2. regrid_weight[c, x, k, j * 128 + y, s] is zero unless s equals y or y + 1; the nonzero weights are positive, and for each destination cell they sum to 1 over k and s.
All inputs are finite; a program needn't handle non-finite values. No bound on the sum of `sea_mask` on one device may be relied on, other than what follows from the above.
Results may differ from a plain program's by a relative error of at most 0.0001.
Values sent between devices are 32-bit elements; how exact they have to be, the bound alone decides.
No kernel may reach another device: no remote copies, remote signals or barrier semaphores. Data moves between devices by JAX's collectives and lax.ppermute only.
A program may use at most 128 MiB of HBM per device.

v0:
```python
import jax
import jax.numpy as jnp
from jax import lax
from jax.sharding import PartitionSpec as P

F = 4
K = 2
SWEEPS = 4


coupling = (0.8, 0.6, 0.4, 0.3)


def from_partner(block, axis, stride):
    count = lax.axis_size(axis)
    route = []
    for low in range(count):
        high = low | 1 << stride
        if high != low and high < count:
            route += [(low, high), (high, low)]
    return lax.ppermute(block, axis, route)


def padded_2(value, sides, width):
    for axis, dim in sides:
        count, length = (lax.axis_size(axis), value.shape[dim])
        up = [(i, (i + 1) % count) for i in range(count - 1)]
        down = [(j, i) for i, j in up]
        last = lax.slice_in_dim(value, length - width, length, axis=dim)
        leading = lax.slice_in_dim(value, 0, width, axis=dim)
        before = lax.ppermute(last, axis, up)
        after = lax.ppermute(leading, axis, down)
        value = jnp.concatenate([before, value, after], axis=dim)
    return value


def thomas(mixing_col, rhs_field):
    depth = rhs_field.shape[0]
    ratios = []
    partial_sol = []
    for layer_id in range(depth):
        if layer_id > 0:
            nu_below = mixing_col[layer_id - 1]
            diagonal = 1.0 + nu_below
        else:
            diagonal = jnp.ones_like(rhs_field[0])
        if layer_id < depth - 1:
            diagonal = diagonal + mixing_col[layer_id]
        if layer_id > 0:
            pivot = diagonal - nu_below * ratios[-1]
            value = (rhs_field[layer_id] + nu_below * partial_sol[-1]) / pivot
        else:
            pivot = diagonal
            value = rhs_field[0] / pivot
        if layer_id < depth - 1:
            ratios.append(mixing_col[layer_id] / pivot)
        else:
            ratios.append(jnp.zeros_like(pivot))
        partial_sol.append(value)
    result = [None] * depth
    result[depth - 1] = partial_sol[depth - 1]
    for layer_id in range(depth - 2, -1, -1):
        result[layer_id] = partial_sol[layer_id] + ratios[layer_id] * result[layer_id + 1]
    return jnp.stack(result)


def advance(padded, kappa, mixing_col, force_field, sea_field):
    centre = padded[:, 1:-1, 1:-1]
    lapl = (
        padded[:, 2:, 1:-1]
        + padded[:, :-2, 1:-1]
        + padded[:, 1:-1, 2:]
        + padded[:, 1:-1, :-2]
        - 4.0 * centre
    )
    rhs_field = centre + kappa * lapl + force_field
    solved = thomas(mixing_col, rhs_field)
    return jnp.where(sea_field > 0.5, solved, centre)


def picker(wanted, carry, piece):
    count = piece.shape[1]
    inside = (wanted >= 0) & (wanted < count)
    taken = piece[:, jnp.clip(wanted, 0, count - 1)]
    return jnp.where(inside[None, :, :, None], taken, carry)


def shards(state, diffusivity, mixing, sea_mask, source_row, regrid_weight):
    comp_id = lax.axis_index("comp")
    atmosphere = comp_id == 0
    block = state[0]
    depth = block.shape[0]
    width_x = block.shape[1]
    width_y = block.shape[2]
    surf = jnp.where(atmosphere, block[depth - F :][::-1], block[:F])
    indices = source_row[0, :, 0, :]
    empty = jnp.zeros((F, width_x, K, width_y), jnp.float32)
    peer = from_partner(surf, "comp", 0)
    picked = picker(indices, empty, lax.all_gather(peer, "gx", axis=1, tiled=True))
    other = jnp.einsum("fxks,xkys->fxy", picked, regrid_weight[0], precision=lax.Precision.HIGHEST)
    total = jnp.zeros((width_x, width_y), jnp.float32)
    for level_id in range(F):
        total = total + coupling[level_id] * jnp.tanh(other[level_id])
    forcing = total - surf[0]
    sea_field = jnp.where(
        atmosphere, jnp.ones((width_x, width_y), jnp.float32), sea_mask.astype(jnp.float32)
    )
    forcing = forcing * sea_field
    target = jnp.where(atmosphere, depth - 1, 0)
    layer_ids = jnp.arange(depth, dtype=jnp.int32)
    level_pick = (layer_ids == target).astype(jnp.float32)[:, None, None]
    kappa = diffusivity[0]
    mixing_col = mixing[0]
    field = block
    force_field = level_pick * forcing
    for sweep_id in range(SWEEPS):
        padded = padded_2(field, (("gx", 1), ("gy", 2)), 1)
        field = advance(padded, kappa, mixing_col, force_field, sea_field)
    return field[None]


def solution(mesh):
    placed = (
        P("comp", None, "gx", "gy"),
        P("comp", "gx", "gy"),
        P("comp", None, "gx", "gy"),
        P("gx", "gy"),
        P("comp", "gx", "gy", None),
        P("comp", "gx", None, "gy", None),
    )
    return jax.shard_map(
        shards, mesh=mesh, in_specs=placed, out_specs=P("comp", None, "gx", "gy"), check_vma=False
    )
```

profile of v0, /device:TPU:3, one launch (start us, length us, event | category | flops | bytes accessed | tf_op | source)
XLA Modules:
  0.0 210.3 jit_solution(14930812674244161627)
XLA Ops:
  8.6 3.0 %collective-permute-start.4 = (f32[4,128,128]{2,1,0:T(8,128)S(1)}, f32[4,128,128]{2,1,0:T(8,128)S(1)}, u32[]{:S(2)}, u32[]{:S(2)}) collective-permute-start(f32[4,128,128]{2,1,0:T(8,128)S(1)} %bitcast_select_fusion), channel_id=1, source_target_pairs={{0,64},{64,0},{1,65},{65,1},{2,66},{66,2},{3,67},{67,3},{4,68},{68... | collective-permute-start | bytes 786440 | tf_op jit(solution)/shard_map/ppermute | solution.py:21
  11.6 5.8 %collective-permute-done.4 = f32[4,128,128]{2,1,0:T(8,128)S(1)} collective-permute-done((f32[4,128,128]{2,1,0:T(8,128)S(1)}, f32[4,128,128]{2,1,0:T(8,128)S(1)}, u32[]{:S(2)}, u32[]{:S(2)}) %collective-permute-start.4) | collective-permute-done | bytes 262176 | tf_op jit(solution)/shard_map/ppermute | solution.py:21
  18.3 5.6 %collective-permute-start = (f32[16,1,128]{2,0,1:T(8,128)S(1)}, f32[16,1,128]{2,0,1:T(8,128)S(1)}, u32[]{:S(2)}, u32[]{:S(2)}) collective-permute-start(f32[16,1,128]{2,0,1:T(8,128)S(1)} %bitcast.689), channel_id=1, source_target_pairs={{4,0},{8,4},{12,8},{16,12},{20,16},{24,20},{28,24},{32,28},{36,32}... | collective-permute-start | bytes 24584 | tf_op jit(solution)/shard_map/ppermute | solution.py:32
  26.2 4.2 %collective-permute-done.1 = f32[16,1,128]{2,0,1:T(8,128)S(1)} collective-permute-done((f32[16,1,128]{2,0,1:T(8,128)S(1)}, f32[16,1,128]{2,0,1:T(8,128)S(1)}, u32[]{:S(2)}, u32[]{:S(2)}) %collective-permute-start.1) | collective-permute-done | bytes 8224 | tf_op jit(solution)/shard_map/ppermute | solution.py:31
  34.4 6.1 %collective-permute-start.3 = (f32[16,130,1]{1,0,2:T(8,128)S(1)}, f32[16,130,1]{1,0,2:T(8,128)S(1)}, u32[]{:S(2)}, u32[]{:S(2)}) collective-permute-start(f32[16,130,1]{1,0,2:T(8,128)S(1)} %copy.168), channel_id=1, source_target_pairs={{0,1},{1,2},{2,3},{4,5},{5,6},{6,7},{8,9},{9,10},{10,11},{12,13},{... | collective-permute-start | bytes 24968 | tf_op jit(solution)/shard_map/ppermute | solution.py:31
  47.3 26.0 %all-gather.2.cloned.1.call-done = f32[4,2048,128]{2,0,1:T(4,128)} async-done(((f32[4,128,128]{2,0,1:T(4,128)}), f32[4,2048,128]{2,0,1:T(4,128)}) %all-gather.2.cloned.1.call-update) | async-done | bytes 4194320 | tf_op jit(solution)/shard_map/all_gather | solution.py:99
  73.3 3.2 %gather_fusion = f32[256,4,128]{2,1,0:T(4,128)S(1)} fusion(f32[4,2048,128]{2,0,1:T(4,128)} %all-gather.2.cloned.1.call-done, s32[1024]{0:T(1024)S(1)} %pad_clamp_fusion), kind=kCustom, calls=%fused_computation | custom fusion | bytes 1049600 | tf_op jit(solution)/shard_map/gather | solution.py:84
  76.6 16.8 %fusion.2 = f32[128,4,128]{2,1,0:T(4,128)S(1)} fusion(f32[1,128,2,128,128]{4,3,2,1,0:T(8,128)} %param.11, f32[128,2,4,128]{3,2,1,0:T(4,128)S(1)} %bitcast.666, pred[128,2]{1,0:T(8,128)(4,1)S(1)} %copy.170), kind=kOutput, calls=%fused_computation.7 | convolution fusion | flops 201457664 | bytes 17563904 | tf_op jit(solution)/shard_map/fxks,xkys->fxy/dot_general | solution.py:100
  97.7 4.3 %collective-permute-start.5 = (f32[16,1,128]{2,0,1:T(8,128)S(1)}, f32[16,1,128]{2,0,1:T(8,128)S(1)}, u32[]{:S(2)}, u32[]{:S(2)}) collective-permute-start(f32[16,1,128]{2,0,1:T(8,128)S(1)} %bitcast.693), channel_id=1, source_target_pairs={{4,0},{8,4},{12,8},{16,12},{20,16},{24,20},{28,24},{32,28},{36,32}... | collective-permute-start | bytes 24584 | tf_op jit(solution)/shard_map/ppermute | solution.py:32
  104.0 4.5 %collective-permute-done.6 = f32[16,1,128]{2,0,1:T(8,128)S(1)} collective-permute-done((f32[16,1,128]{2,0,1:T(8,128)S(1)}, f32[16,1,128]{2,0,1:T(8,128)S(1)}, u32[]{:S(2)}, u32[]{:S(2)}) %collective-permute-start.6) | collective-permute-done | bytes 8224 | tf_op jit(solution)/shard_map/ppermute | solution.py:31
  110.9 2.4 %copy.180 = f32[16,130,1]{1,0,2:T(8,128)} copy(f32[16,130,1]{2,1,0:T(8,128)} %get-tuple-element.151) | data formatting | bytes 16640 | tf_op jit(solution)/shard_map/slice | solution.py:30
  113.4 2.4 %copy.182 = f32[16,130,1]{1,0,2:T(8,128)} copy(f32[16,130,1]{2,1,0:T(8,128)} %get-tuple-element.152) | data formatting | bytes 16640 | tf_op jit(solution)/shard_map/slice | solution.py:29
  115.8 5.1 %collective-permute-start.8 = (f32[16,130,1]{1,0,2:T(8,128)}, f32[16,130,1]{1,0,2:T(8,128)}, u32[]{:S(2)}, u32[]{:S(2)}) collective-permute-start(f32[16,130,1]{1,0,2:T(8,128)} %copy.182), channel_id=1, source_target_pairs={{0,1},{1,2},{2,3},{4,5},{5,6},{6,7},{8,9},{9,10},{10,11},{12,13},{... | collective-permute-start | bytes 24968 | tf_op jit(solution)/shard_map/ppermute | solution.py:31
  130.7 2.7 %multiply_add_fusion.2 = f32[16,128,128]{2,1,0:T(8,128)S(1)} fusion(f32[16,128,128]{2,1,0:T(8,128)S(1)} %broadcast_select_fusion.2, f32[16,130,1]{2,1,0:T(8,128)} %copy.183, f32[16,1,128]{2,1,0:T(1,128)} %bitcast.681, f32[16,1,128]{2,1,0:T(1,128)} %bitcast.685, f32[16,130,1]{2,1,0:T(8,128)} %copy.181, f32[128,128]{1,0:T(8,128)} %copy-done.9, ...), kind=kLoop, calls=%fused_computation.5 | loop fusion | flops 4456448 | bytes 2261312 | tf_op jit(solution)/shard_map/add | solution.py:76
  138.3 3.4 %collective-permute-start.10 = (f32[16,1,128]{2,0,1:T(8,128)S(1)}, f32[16,1,128]{2,0,1:T(8,128)S(1)}, u32[]{:S(2)}, u32[]{:S(2)}) collective-permute-start(f32[16,1,128]{2,0,1:T(8,128)S(1)} %bitcast.691), channel_id=1, source_target_pairs={{0,4},{4,8},{8,12},{12,16},{16,20},{20,24},{24,28},{28,32},{32,36}... | collective-permute-start | bytes 24584 | tf_op jit(solution)/shard_map/ppermute | solution.py:31
  141.8 3.1 %collective-permute-done.10 = f32[16,1,128]{2,0,1:T(8,128)S(1)} collective-permute-done((f32[16,1,128]{2,0,1:T(8,128)S(1)}, f32[16,1,128]{2,0,1:T(8,128)S(1)}, u32[]{:S(2)}, u32[]{:S(2)}) %collective-permute-start.10) | collective-permute-done | bytes 8224 | tf_op jit(solution)/shard_map/ppermute | solution.py:31
  146.7 2.4 %copy.190 = f32[16,130,1]{1,0,2:T(8,128)} copy(f32[16,130,1]{2,1,0:T(8,128)} %get-tuple-element.149) | data formatting | bytes 16640 | tf_op jit(solution)/shard_map/slice | solution.py:30
  149.1 2.5 %copy.192 = f32[16,130,1]{1,0,2:T(8,128)} copy(f32[16,130,1]{2,1,0:T(8,128)} %get-tuple-element.150) | data formatting | bytes 16640 | tf_op jit(solution)/shard_map/slice | solution.py:29
  151.6 3.0 %collective-permute-start.12 = (f32[16,130,1]{1,0,2:T(8,128)}, f32[16,130,1]{1,0,2:T(8,128)}, u32[]{:S(2)}, u32[]{:S(2)}) collective-permute-start(f32[16,130,1]{1,0,2:T(8,128)} %copy.192), channel_id=1, source_target_pairs={{0,1},{1,2},{2,3},{4,5},{5,6},{6,7},{8,9},{9,10},{10,11},{12,13},{... | collective-permute-start | bytes 24968 | tf_op jit(solution)/shard_map/ppermute | solution.py:31
  164.3 2.7 %multiply_add_fusion.1 = f32[16,128,128]{2,1,0:T(8,128)S(1)} fusion(f32[16,128,128]{2,1,0:T(8,128)S(1)} %broadcast_select_fusion.1, f32[16,130,1]{2,1,0:T(8,128)} %copy.193, f32[16,1,128]{2,1,0:T(1,128)} %bitcast.683, f32[16,1,128]{2,1,0:T(1,128)} %bitcast.687, f32[16,130,1]{2,1,0:T(8,128)} %copy.191, f32[128,128]{1,0:T(8,128)} %copy-done.9, ...), kind=kLoop, calls=%fused_computation.4 | loop fusion | flops 4456448 | bytes 2261312 | tf_op jit(solution)/shard_map/add | solution.py:76
  171.2 3.4 %collective-permute-start.14 = (f32[16,1,128]{2,0,1:T(8,128)S(1)}, f32[16,1,128]{2,0,1:T(8,128)S(1)}, u32[]{:S(2)}, u32[]{:S(2)}) collective-permute-start(f32[16,1,128]{2,0,1:T(8,128)S(1)} %bitcast.692), channel_id=1, source_target_pairs={{0,4},{4,8},{8,12},{12,16},{16,20},{20,24},{24,28},{28,32},{32,36}... | collective-permute-start | bytes 24584 | tf_op jit(solution)/shard_map/ppermute | solution.py:31
  174.6 3.1 %collective-permute-done.14 = f32[16,1,128]{2,0,1:T(8,128)S(1)} collective-permute-done((f32[16,1,128]{2,0,1:T(8,128)S(1)}, f32[16,1,128]{2,0,1:T(8,128)S(1)}, u32[]{:S(2)}, u32[]{:S(2)}) %collective-permute-start.14) | collective-permute-done | bytes 8224 | tf_op jit(solution)/shard_map/ppermute | solution.py:31
  183.4 3.0 %collective-permute-start.16 = (f32[16,130,1]{1,0,2:T(8,128)}, f32[16,130,1]{1,0,2:T(8,128)}, u32[]{:S(2)}, u32[]{:S(2)}) collective-permute-start(f32[16,130,1]{1,0,2:T(8,128)} %copy.202), channel_id=1, source_target_pairs={{0,1},{1,2},{2,3},{4,5},{5,6},{6,7},{8,9},{9,10},{10,11},{12,13},{... | collective-permute-start | bytes 24968 | tf_op jit(solution)/shard_map/ppermute | solution.py:31
  196.2 2.7 %multiply_add_fusion = f32[16,128,128]{2,1,0:T(8,128)S(1)} fusion(f32[16,128,128]{2,1,0:T(8,128)S(1)} %copy-done.5, f32[16,130,1]{2,1,0:T(8,128)} %copy.203, f32[16,1,128]{2,1,0:T(1,128)} %bitcast.677, f32[16,1,128]{2,1,0:T(1,128)} %bitcast.679, f32[16,130,1]{2,1,0:T(8,128)} %copy.201, f32[128,128]{1,0:T(8,128)S(1)} %copy-done.10, f32[16]{0:T(128)} %compare_convert_fusion, ...), kind=kLoop, calls=%fused_computation.3 | loop fusion | flops 4456448 | bytes 2261312 | tf_op jit(solution)/shard_map/add | solution.py:76
  (406 shorter events, 73.2 us)
Async XLA Ops:
  6.5 19.3 %copy-start.113 = (s32[1,128,1,2]{1,3,2,0:T(2,128)S(1)}, s32[1,128,1,2]{1,3,2,0:T(2,128)}, u32[]{:S(2)}) copy-start(s32[1,128,1,2]{1,3,2,0:T(2,128)} %param.10) | copy-start | bytes 3076
  6.5 66.8 %all-gather.2.cloned.1.call-start = ((), (), s32[]{:S(2)}) async-start(), calls=%async_computation | async-start | bytes 4456448 | tf_op jit(solution)/shard_map/all_gather | solution.py:99
  6.5 19.6 %copy-start.101 = (s32[128,128]{1,0:T(8,128)S(1)}, s32[128,128]{1,0:T(8,128)}, u32[]{:S(2)}) copy-start(s32[128,128]{1,0:T(8,128)} %param.9) | copy-start | bytes 196612
  8.6 8.8 %collective-permute-start.4 = (f32[4,128,128]{2,1,0:T(8,128)S(1)}, f32[4,128,128]{2,1,0:T(8,128)S(1)}, u32[]{:S(2)}, u32[]{:S(2)}) collective-permute-start(f32[4,128,128]{2,1,0:T(8,128)S(1)} %bitcast_select_fusion), channel_id=1, source_target_pairs={{0,64},{64,0},{1,65},{65,1},{2,66},{66,2},{3,67},{67,3},{4,68},{68... | collective-permute-start | bytes 786440 | tf_op jit(solution)/shard_map/ppermute | solution.py:21
  18.3 7.9 %collective-permute-start = (f32[16,1,128]{2,0,1:T(8,128)S(1)}, f32[16,1,128]{2,0,1:T(8,128)S(1)}, u32[]{:S(2)}, u32[]{:S(2)}) collective-permute-start(f32[16,1,128]{2,0,1:T(8,128)S(1)} %bitcast.689), channel_id=1, source_target_pairs={{4,0},{8,4},{12,8},{16,12},{20,16},{24,20},{28,24},{32,28},{36,32}... | collective-permute-start | bytes 24584 | tf_op jit(solution)/shard_map/ppermute | solution.py:32
  23.9 6.5 %collective-permute-start.1 = (f32[16,1,128]{2,0,1:T(8,128)S(1)}, f32[16,1,128]{2,0,1:T(8,128)S(1)}, u32[]{:S(2)}, u32[]{:S(2)}) collective-permute-start(f32[16,1,128]{2,0,1:T(8,128)S(1)} %bitcast.688), channel_id=1, source_target_pairs={{0,4},{4,8},{8,12},{12,16},{16,20},{20,24},{24,28},{28,32},{32,36}... | collective-permute-start | bytes 24584 | tf_op jit(solution)/shard_map/ppermute | solution.py:31
  34.4 11.6 %collective-permute-start.3 = (f32[16,130,1]{1,0,2:T(8,128)S(1)}, f32[16,130,1]{1,0,2:T(8,128)S(1)}, u32[]{:S(2)}, u32[]{:S(2)}) collective-permute-start(f32[16,130,1]{1,0,2:T(8,128)S(1)} %copy.168), channel_id=1, source_target_pairs={{0,1},{1,2},{2,3},{4,5},{5,6},{6,7},{8,9},{9,10},{10,11},{12,13},{... | collective-permute-start | bytes 24968 | tf_op jit(solution)/shard_map/ppermute | solution.py:31
  40.4 5.1 %collective-permute-start.2 = (f32[16,130,1]{1,0,2:T(8,128)S(1)}, f32[16,130,1]{1,0,2:T(8,128)S(1)}, u32[]{:S(2)}, u32[]{:S(2)}) collective-permute-start(f32[16,130,1]{1,0,2:T(8,128)S(1)} %copy.166), channel_id=1, source_target_pairs={{1,0},{2,1},{3,2},{5,4},{6,5},{7,6},{9,8},{10,9},{11,10},{13,12},{... | collective-permute-start | bytes 24968 | tf_op jit(solution)/shard_map/ppermute | solution.py:32
  76.5 17.0 %copy-start.6 = (f32[16,130,1]{2,1,0:T(8,128)S(1)}, f32[16,130,1]{2,1,0:T(8,128)}, u32[]{:S(2)}) copy-start(f32[16,130,1]{2,1,0:T(8,128)} %copy.169) | copy-start | bytes 24964
  76.5 17.0 %copy-start.52 = (f32[1,128,128]{2,1,0:T(8,128)S(1)}, f32[1,128,128]{2,1,0:T(8,128)}, u32[]{:S(2)}) copy-start(f32[1,128,128]{2,1,0:T(8,128)} %param.7) | copy-start | bytes 196612
  95.9 71.5 %copy-start.7 = (f32[1,128,128]{2,1,0:T(8,128)}, f32[1,128,128]{2,1,0:T(8,128)S(1)}, u32[]{:S(2)}) copy-start(f32[1,128,128]{2,1,0:T(8,128)S(1)} %get-tuple-element.141) | copy-start | bytes 196612
  97.7 32.9 %copy-start.2 = (f32[16,128,128]{2,1,0:T(8,128)}, f32[16,128,128]{2,1,0:T(8,128)S(1)}, u32[]{:S(2)}) copy-start(f32[16,128,128]{2,1,0:T(8,128)S(1)} %broadcast_select_fusion.2) | copy-start | bytes 3145732
  97.7 6.3 %collective-permute-start.5 = (f32[16,1,128]{2,0,1:T(8,128)S(1)}, f32[16,1,128]{2,0,1:T(8,128)S(1)}, u32[]{:S(2)}, u32[]{:S(2)}) collective-permute-start(f32[16,1,128]{2,0,1:T(8,128)S(1)} %bitcast.693), channel_id=1, source_target_pairs={{4,0},{8,4},{12,8},{16,12},{20,16},{24,20},{28,24},{32,28},{36,32}... | collective-permute-start | bytes 24584 | tf_op jit(solution)/shard_map/ppermute | solution.py:32
  102.0 6.5 %collective-permute-start.6 = (f32[16,1,128]{2,0,1:T(8,128)S(1)}, f32[16,1,128]{2,0,1:T(8,128)S(1)}, u32[]{:S(2)}, u32[]{:S(2)}) collective-permute-start(f32[16,1,128]{2,0,1:T(8,128)S(1)} %bitcast.690), channel_id=1, source_target_pairs={{0,4},{4,8},{8,12},{12,16},{16,20},{20,24},{24,28},{28,32},{32,36}... | collective-permute-start | bytes 24584 | tf_op jit(solution)/shard_map/ppermute | solution.py:31
  115.8 12.6 %collective-permute-start.8 = (f32[16,130,1]{1,0,2:T(8,128)}, f32[16,130,1]{1,0,2:T(8,128)}, u32[]{:S(2)}, u32[]{:S(2)}) collective-permute-start(f32[16,130,1]{1,0,2:T(8,128)} %copy.182), channel_id=1, source_target_pairs={{0,1},{1,2},{2,3},{4,5},{5,6},{6,7},{8,9},{9,10},{10,11},{12,13},{... | collective-permute-start | bytes 24968 | tf_op jit(solution)/shard_map/ppermute | solution.py:31
  120.9 5.4 %collective-permute-start.7 = (f32[16,130,1]{1,0,2:T(8,128)}, f32[16,130,1]{1,0,2:T(8,128)}, u32[]{:S(2)}, u32[]{:S(2)}) collective-permute-start(f32[16,130,1]{1,0,2:T(8,128)} %copy.180), channel_id=1, source_target_pairs={{1,0},{2,1},{3,2},{5,4},{6,5},{7,6},{9,8},{10,9},{11,10},{13,12},{... | collective-permute-start | bytes 24968 | tf_op jit(solution)/shard_map/ppermute | solution.py:32
  136.4 5.3 %collective-permute-start.9 = (f32[16,1,128]{2,0,1:T(8,128)S(1)}, f32[16,1,128]{2,0,1:T(8,128)S(1)}, u32[]{:S(2)}, u32[]{:S(2)}) collective-permute-start(f32[16,1,128]{2,0,1:T(8,128)S(1)} %bitcast.694), channel_id=1, source_target_pairs={{4,0},{8,4},{12,8},{16,12},{20,16},{24,20},{28,24},{32,28},{36,32}... | collective-permute-start | bytes 24584 | tf_op jit(solution)/shard_map/ppermute | solution.py:32
  138.3 6.5 %collective-permute-start.10 = (f32[16,1,128]{2,0,1:T(8,128)S(1)}, f32[16,1,128]{2,0,1:T(8,128)S(1)}, u32[]{:S(2)}, u32[]{:S(2)}) collective-permute-start(f32[16,1,128]{2,0,1:T(8,128)S(1)} %bitcast.691), channel_id=1, source_target_pairs={{0,4},{4,8},{8,12},{12,16},{16,20},{20,24},{24,28},{28,32},{32,36}... | collective-permute-start | bytes 24584 | tf_op jit(solution)/shard_map/ppermute | solution.py:31
  151.6 10.5 %collective-permute-start.12 = (f32[16,130,1]{1,0,2:T(8,128)}, f32[16,130,1]{1,0,2:T(8,128)}, u32[]{:S(2)}, u32[]{:S(2)}) collective-permute-start(f32[16,130,1]{1,0,2:T(8,128)} %copy.192), channel_id=1, source_target_pairs={{0,1},{1,2},{2,3},{4,5},{5,6},{6,7},{8,9},{9,10},{10,11},{12,13},{... | collective-permute-start | bytes 24968 | tf_op jit(solution)/shard_map/ppermute | solution.py:31
  154.6 5.4 %collective-permute-start.11 = (f32[16,130,1]{1,0,2:T(8,128)}, f32[16,130,1]{1,0,2:T(8,128)}, u32[]{:S(2)}, u32[]{:S(2)}) collective-permute-start(f32[16,130,1]{1,0,2:T(8,128)} %copy.190), channel_id=1, source_target_pairs={{1,0},{2,1},{3,2},{5,4},{6,5},{7,6},{9,8},{10,9},{11,10},{13,12},{... | collective-permute-start | bytes 24968 | tf_op jit(solution)/shard_map/ppermute | solution.py:32
  169.3 5.3 %collective-permute-start.13 = (f32[16,1,128]{2,0,1:T(8,128)S(1)}, f32[16,1,128]{2,0,1:T(8,128)S(1)}, u32[]{:S(2)}, u32[]{:S(2)}) collective-permute-start(f32[16,1,128]{2,0,1:T(8,128)S(1)} %bitcast.695), channel_id=1, source_target_pairs={{4,0},{8,4},{12,8},{16,12},{20,16},{24,20},{28,24},{32,28},{36,32}... | collective-permute-start | bytes 24584 | tf_op jit(solution)/shard_map/ppermute | solution.py:32
  171.2 6.5 %collective-permute-start.14 = (f32[16,1,128]{2,0,1:T(8,128)S(1)}, f32[16,1,128]{2,0,1:T(8,128)S(1)}, u32[]{:S(2)}, u32[]{:S(2)}) collective-permute-start(f32[16,1,128]{2,0,1:T(8,128)S(1)} %bitcast.692), channel_id=1, source_target_pairs={{0,4},{4,8},{8,12},{12,16},{16,20},{20,24},{24,28},{28,32},{32,36}... | collective-permute-start | bytes 24584 | tf_op jit(solution)/shard_map/ppermute | solution.py:31
  183.4 10.5 %collective-permute-start.16 = (f32[16,130,1]{1,0,2:T(8,128)}, f32[16,130,1]{1,0,2:T(8,128)}, u32[]{:S(2)}, u32[]{:S(2)}) collective-permute-start(f32[16,130,1]{1,0,2:T(8,128)} %copy.202), channel_id=1, source_target_pairs={{0,1},{1,2},{2,3},{4,5},{5,6},{6,7},{8,9},{9,10},{10,11},{12,13},{... | collective-permute-start | bytes 24968 | tf_op jit(solution)/shard_map/ppermute | solution.py:31
  186.4 5.4 %collective-permute-start.15 = (f32[16,130,1]{1,0,2:T(8,128)}, f32[16,130,1]{1,0,2:T(8,128)}, u32[]{:S(2)}, u32[]{:S(2)}) collective-permute-start(f32[16,130,1]{1,0,2:T(8,128)} %copy.200), channel_id=1, source_target_pairs={{1,0},{2,1},{3,2},{5,4},{6,5},{7,6},{9,8},{10,9},{11,10},{13,12},{... | collective-permute-start | bytes 24968 | tf_op jit(solution)/shard_map/ppermute | solution.py:32
  (108 other events, 281.6 us)
Sparse Core Ops, SparseCore 0:
  18.4 54.8 all-gather.1
where the time goes:
time: 212 us; the launch traced here: 210 us
  waiting for transfers between devices  54.8 us (26%)
  local copies, waits for them, and re-layouts  54.3 us (26%)
  starting transfers between devices  52.3 us (25%)
  matrix products  16.8 us (8%)
  other arithmetic  16.3 us (8%)
  between operations  15.7 us (7%)
    ppermute x8, starting transfers between devices, padded_2(): before = lax.ppermute(last, axis, up)  27.7 us
    all_gather x1, waiting for transfers between devices, shards(): lax.all_gather(peer, 'gx', axis=1, tiled=True)  26 us
    ppermute x8, starting transfers between devices, padded_2(): after = lax.ppermute(leading, axis, down)  21.7 us
    dot_general x1, matrix products, shards(): jnp.einsum('fxks,xkys->fxy', picked, regrid_weight[0], precision=lax.Prec...  16.8 us
    slice x8, local copies, waits for them, and re-layouts, padded_2(): leading = lax.slice_in_dim(value, 0, width, axis=dim)  15.3 us
    ppermute x8, waiting for transfers between devices, padded_2(): before = lax.ppermute(last, axis, up)  14.9 us
    unnamed x319, local copies, waits for them, and re-layouts  10.4 us
    add x4, other arithmetic, advance(): rhs_field = centre + kappa * lapl + force_field  9.35 us
  transfers between devices with their start and end apart: 18, of which 10 were waited for; matrix products, arithmetic and copies ran while one was open for 8% of the time, Pallas kernels for 0%

commit v1 on v0

v1 whole, which is shorter than its diff:
```python
import functools

import jax
import jax.numpy as jnp
from jax import lax
from jax.experimental import pallas as pl
from jax.experimental.pallas import tpu as pltpu
from jax.sharding import PartitionSpec as P

F = 4
SWEEPS = 4
LEV = 16
N = 128
HALO = 8
ROWS = N + 2 * HALO
GX = 16
UNIT = 64

coupling = (0.8, 0.6, 0.4, 0.3)

f32 = jnp.float32
VMEM = pl.BlockSpec(memory_space=pltpu.VMEM)
SMEM = pl.BlockSpec(memory_space=pltpu.SMEM)

PACK = (
    [(4 * q, 4) for q in range(LEV)]
    + [(64 + 3 * i, 3) for i in range(LEV - 1)]
    + [(109, 3), (112, 3)]
)


def params(vmem_mib):
    return pltpu.CompilerParams(vmem_limit_bytes=vmem_mib * 2**20)


def band_kernel(w_ref, out_ref):
    rows = w_ref.shape[0]
    sub = lax.broadcasted_iota(jnp.int32, (8, N), 0)
    lane = lax.broadcasted_iota(jnp.int32, (8, N), 1)
    same = sub == lane % 8
    after = sub == (lane + 7) % 8
    for k in range(2):
        own, nxt = [], []
        for x in range(rows):
            tile = w_ref[x, k, 0:8, :]
            for i in range(1, N // 8):
                tile = tile + w_ref[x, k, 8 * i : 8 * i + 8, :]
            own.append(jnp.sum(jnp.where(same, tile, 0.0), axis=0, keepdims=True))
            nxt.append(jnp.sum(jnp.where(after, tile, 0.0), axis=0, keepdims=True))
        out_ref[k] = jnp.concatenate(own, axis=0)
        out_ref[2 + k] = jnp.concatenate(nxt, axis=0)


def band(weight):
    step = 8
    return pl.pallas_call(
        band_kernel,
        grid=(N // step,),
        in_specs=[pl.BlockSpec((step, 2, N, N), lambda i: (i, 0, 0, 0))],
        out_specs=pl.BlockSpec((4, step, N), lambda i: (0, i, 0)),
        out_shape=jax.ShapeDtypeStruct((4, N, N), f32),
        compiler_params=params(56),
        cost_estimate=pl.CostEstimate(flops=2**22, bytes_accessed=2**24, transcendentals=0),
        name="band",
    )(weight)


def edge_kernel(par, state, mixing, kappa, mask, top, bottom):
    ocean = par[0] == 1
    for out, low in ((top, 0), (bottom, N - HALO)):
        rows = slice(low, low + HALO)
        sea = jnp.where(ocean, mask[rows].astype(f32), 1.0)
        for level in range(LEV):
            out[level] = state[level, rows]
        for level in range(LEV - 1):
            out[LEV + level] = mixing[level, rows] * sea
        out[2 * LEV - 1] = kappa[rows] * sea


def edges(par, state, mixing, kappa, mask):
    shape = jax.ShapeDtypeStruct((2 * LEV, HALO, N), f32)
    return pl.pallas_call(
        edge_kernel,
        in_specs=[SMEM] + [VMEM] * 4,
        out_specs=[VMEM, VMEM],
        out_shape=[shape, shape],
        compiler_params=params(16),
        name="edges",
    )(par, state, mixing, kappa, mask)


def force_kernel(par, a, b, c1, c2, diag, surf, mask, out, window, rows):
    comp, x, e, units = par[0], par[1], par[2], par[3]

    @pl.when(comp == 1)
    def _():
        odd = units % 2
        low = x < 8
        take_1 = low == (odd == 1)
        base = odd * UNIT
        at_a = pl.multiple_of(jnp.where(low, base, base + N), UNIT)
        at_b = pl.multiple_of(jnp.where(low, base + N, base), UNIT)
        at_c = pl.multiple_of((1 - odd) * 2 * N, UNIT)
        window[:, pl.ds(at_a, N), :] = a[...]
        window[:, pl.ds(at_b, N), :] = b[...]
        window[:, pl.ds(at_c, UNIT), :] = jnp.where(take_1, c1[...], c2[...])
        for f in range(F):
            for k in range(2):
                rows[k, f] = window[f, pl.ds(e + k, N, stride=2), :]

    @pl.when(comp == 0)
    def _():
        odd = (x + units) % 2

        @pl.when(odd == 0)
        def _():
            window[:, 0:N, :] = a[...]

        @pl.when(odd == 1)
        def _():
            window[:, 0:UNIT, :] = c1[...]
            window[:, UNIT:N, :] = c2[...]

        for f in range(F):
            for k in range(2):
                half = window[f, pl.ds(e + k, UNIT), :]
                rows[k, f, pl.ds(0, UNIT, stride=2), :] = half
                rows[k, f, pl.ds(1, UNIT, stride=2), :] = half

    total = jnp.zeros((N, N), f32)
    for i in range(F):
        scale = jnp.where(comp == 1, coupling[F - 1 - i], coupling[i])
        r0 = rows[0, i]
        r1 = rows[1, i]
        after = diag[2] * r0 + diag[3] * r1
        value = diag[0] * r0 + diag[1] * r1 + pltpu.roll(after, N - 1, 1)
        total = total + scale * jnp.tanh(value)
    own = surf[jnp.where(comp == 1, 0, F - 1)]
    sea = jnp.where(comp == 1, mask[...].astype(f32), 1.0)
    out[...] = (total - own) * sea


def force(par, pieces, diag, surf, mask):
    return pl.pallas_call(
        force_kernel,
        in_specs=[SMEM] + [VMEM] * 7,
        out_specs=VMEM,
        out_shape=jax.ShapeDtypeStruct((N, N), f32),
        scratch_shapes=[pltpu.VMEM((F, 5 * UNIT + 8, N), f32), pltpu.VMEM((2, F, N, N), f32)],
        compiler_params=params(16),
        name="force",
    )(par, *pieces, diag, surf, mask)


def column_kernel(par, state, mixing, kappa, mask, top, bottom, forcing, f_top, f_bottom, left, right, sea):
    ocean = par[0] == 1
    sea[...] = jnp.where(ocean, mask[...].astype(f32), 1.0)
    lane = lax.broadcasted_iota(jnp.int32, (8, N), 1)
    place = [(lane >= at) & (lane < at + width) for at, width in PACK]

    def tile(get):
        first = jnp.zeros((8, N), f32)
        last = jnp.zeros((8, N), f32)
        for q, (at, width) in enumerate(PACK):
            value = get(q)
            first = jnp.where(place[q], pltpu.roll(value, at, 1), first)
            last = jnp.where(place[q], pltpu.roll(value, (at + width) % N, 1), last)
        return first, last

    def ends(halo, f_halo, rows):
        left[rows], right[rows] = tile(lambda q: halo[q] if q < 2 * LEV else f_halo[...])

    ends(top, f_top, slice(0, HALO))
    ends(bottom, f_bottom, slice(HALO + N, ROWS))

    def body(t, carry):
        rows = pl.ds(pl.multiple_of(t * 8, 8), 8)
        s = sea[rows]

        def get(q):
            if q < LEV:
                return state[q, rows]
            if q < 2 * LEV - 1:
                return mixing[q - LEV, rows] * s
            if q < 2 * LEV:
                return kappa[rows] * s
            return forcing[rows]

        first, last = tile(get)
        out = pl.ds(pl.multiple_of(HALO + t * 8, 8), 8)
        left[out] = first
        right[out] = last
        return carry

    lax.fori_loop(0, N // 8, body, 0)


def columns(par, *arrays):
    shape = jax.ShapeDtypeStruct((ROWS, N), f32)
    return pl.pallas_call(
        column_kernel,
        in_specs=[SMEM] + [VMEM] * 9,
        out_specs=[VMEM, VMEM],
        out_shape=[shape, shape],
        scratch_shapes=[pltpu.VMEM((N, N), f32)],
        compiler_params=params(16),
        name="columns",
    )(par, *arrays)


PAD = ROWS + 16
BLOCK = 16


def sweep_kernel(
    par, state, mixing, kappa, mask, top, bottom, forcing, f_top, f_bottom, left, right, out,
    ua, ub, inv, below, above, kap, frc,
):
    ocean = par[0] == 1
    lane = lax.broadcasted_iota(jnp.int32, (8, N), 1)
    zero = jnp.zeros((8, 2 * N), f32)
    for u in (ua, ub):
        for level in range(LEV):
            u[level, 0:8] = zero
            u[level, PAD - 8 : PAD] = zero

    def setup(get, package_rows, rows):
        pl_ = left[package_rows]
        pr = right[package_rows]

        def field(q):
            at, width = PACK[q]
            after = pltpu.roll(pl_, (N - at) % N, 1)
            before = pltpu.roll(pr, (2 * N - at - width) % N, 1)
            side = jnp.where(lane < width, after, jnp.where(lane >= N - width, before, 0.0))
            return jnp.concatenate([get(q), side], axis=1)

        for level in range(LEV):
            ua[level, rows] = field(level)
        kap[rows] = field(2 * LEV - 1)
        frc[rows] = field(2 * LEV)
        nu_before = None
        ratio = None
        for level in range(LEV):
            pivot = jnp.ones((8, 2 * N), f32)
            if level > 0:
                pivot = pivot + nu_before
            if level < LEV - 1:
                nu = field(LEV + level)
                pivot = pivot + nu
            if level > 0:
                pivot = pivot - nu_before * ratio
            r = 1.0 / pivot
            inv[level, rows] = r
            if level > 0:
                below[level, rows] = nu_before * r
            if level < LEV - 1:
                ratio = nu * r
                above[level, rows] = ratio
                nu_before = nu

    def ends(halo, f_halo, package_rows, rows):
        setup(lambda q: halo[q] if q < 2 * LEV else f_halo[...], package_rows, rows)

    ends(top, f_top, slice(0, 8), slice(8, 16))
    ends(bottom, f_bottom, slice(HALO + N, ROWS), slice(HALO + N + 8, ROWS + 8))

    def build(t, carry):
        src = pl.ds(pl.multiple_of(t * 8, 8), 8)
        s = jnp.where(ocean, mask[src].astype(f32), 1.0)

        def get(q):
            if q < LEV:
                return state[q, src]
            if q < 2 * LEV - 1:
                return mixing[q - LEV, src] * s
            if q < 2 * LEV:
                return kappa[src] * s
            return forcing[src]

        setup(
            get,
            pl.ds(pl.multiple_of(HALO + t * 8, 8), 8),
            pl.ds(pl.multiple_of(HALO + 8 + t * 8, 8), 8),
        )
        return carry

    lax.fori_loop(0, N // 8, build, 0)

    top_force = jnp.where(ocean, 1.0, 0.0)
    bottom_force = jnp.where(ocean, 0.0, 1.0)
    first_row = lax.broadcasted_iota(jnp.int32, (8, 2 * N), 0) == 0
    last_row = lax.broadcasted_iota(jnp.int32, (8, 2 * N), 0) == 7

    def solve(u, base, store):
        tiles = range(BLOCK // 8)
        rows = [pl.ds(pl.multiple_of(base + 8 * i, 8), 8) for i in tiles]
        before = pl.ds(pl.multiple_of(base - 8, 8), 8)
        behind = pl.ds(pl.multiple_of(base + BLOCK, 8), 8)
        k = [kap[r] for r in rows]
        keep = [1.0 - 4.0 * x for x in k]
        part = []
        for level in range(LEV):
            c = [u[level, r] for r in rows]
            around = [u[level, before]] + c + [u[level, behind]]
            row = []
            for i in tiles:
                up = pltpu.roll(jnp.where(last_row, around[i], c[i]), 1, 0)
                down = pltpu.roll(jnp.where(first_row, around[i + 2], c[i]), 7, 0)
                sides = pltpu.roll(c[i], 1, 1) + pltpu.roll(c[i], 2 * N - 1, 1)
                rhs = keep[i] * c[i] + k[i] * ((up + down) + sides)
                if level == 0:
                    rhs = rhs + top_force * frc[rows[i]]
                if level == LEV - 1:
                    rhs = rhs + bottom_force * frc[rows[i]]
                value = rhs * inv[level, rows[i]]
                if level > 0:
                    value = value + below[level, rows[i]] * part[-1][i]
                row.append(value)
            part.append(row)
        v = part[LEV - 1]
        for i in tiles:
            store(LEV - 1, i, v[i])
        for level in range(LEV - 2, -1, -1):
            v = [part[level][i] + above[level, rows[i]] * v[i] for i in tiles]
            for i in tiles:
                store(level, i, v[i])

    for s in range(SWEEPS):
        src, dst = (ua, ub) if s % 2 == 0 else (ub, ua)
        if s < SWEEPS - 1:

            def body(t, carry, src=src, dst=dst):
                base = pl.multiple_of(t * BLOCK + 8, 8)

                def store(level, i, v):
                    dst[level, pl.ds(pl.multiple_of(base + 8 * i, 8), 8)] = v

                solve(src, base, store)
                return carry

            lax.fori_loop(0, ROWS // BLOCK, body, 0)
        else:

            def body(t, carry, src=src):
                base = pl.multiple_of(t * BLOCK + 16, 8)
                o = pl.multiple_of(t * BLOCK, 8)

                def store(level, i, v):
                    out[level, pl.ds(pl.multiple_of(o + 8 * i, 8), 8)] = v[:, :N]

                solve(src, base, store)
                return carry

            lax.fori_loop(0, N // BLOCK, body, 0)


def sweeps(par, *arrays):
    wide = pltpu.VMEM((LEV, PAD, 2 * N), f32)
    return pl.pallas_call(
        sweep_kernel,
        in_specs=[SMEM] + [VMEM] * 11,
        out_specs=VMEM,
        out_shape=jax.ShapeDtypeStruct((LEV, N, N), f32),
        scratch_shapes=[wide] * 5 + [pltpu.VMEM((PAD, 2 * N), f32)] * 2,
        compiler_params=params(40),
        name="sweeps",
    )(par, *arrays)


def shift_pair(low_edge, high_edge, axis):
    count = lax.axis_size(axis)
    up = [(i, i + 1) for i in range(count - 1)]
    down = [(i + 1, i) for i in range(count - 1)]
    return lax.ppermute(high_edge, axis, up), lax.ppermute(low_edge, axis, down)


BOTH = ("comp", "gx")


def routed(block, route):
    route = route % 32
    pairs = [
        (GX + (2 * x + route % GX + ((x >= 8) != (route >= GX))) % GX, GX + x) for x in range(GX)
    ]
    pairs += [((x + route) // 2 % GX, x) for x in range(GX) if (x + route) % 2 == 0]
    return lax.ppermute(block, BOTH, pairs)


def ocean_route(units):
    base = units // 2
    odd = units % 2

    def run(peer):
        whole = (base + odd) % GX
        part = (base + 1 - odd) % GX
        half = peer[:, UNIT:] if odd else peer[:, :UNIT]
        return (
            routed(peer, whole),
            routed(peer, GX + whole),
            routed(half, part),
            routed(half, GX + part),
        )

    return run


def atmosphere_route(units):
    def run(peer):
        return (
            routed(peer, units),
            peer,
            routed(peer[:, UNIT:], units - 1),
            routed(peer[:, :UNIT], units + 1),
        )

    return run


def shards(state, diffusivity, mixing, sea_mask, source_row, regrid_weight):
    comp = lax.axis_index("comp")
    gx = lax.axis_index("gx")
    field = state[0]
    mix = mixing[0]
    kappa = diffusivity[0]
    surf = lax.dynamic_slice(field, ((LEV - F) * (1 - comp), 0, 0), (F, N, N))
    swap = [(x, GX + x) for x in range(GX)] + [(GX + x, x) for x in range(GX)]
    peer = lax.ppermute(surf, BOTH, swap)
    first = source_row[0, 0, 0, 0]
    units = jnp.where(comp == 1, first // UNIT - 4 * gx, first // UNIT - gx) % 32
    par = jnp.stack([comp, gx, first % UNIT, units]).astype(jnp.int32)
    diag = band(regrid_weight[0])
    top, bottom = shift_pair(*edges(par, field, mix, kappa, sea_mask), "gx")
    peer, diag, top, bottom = lax.optimization_barrier((peer, diag, top, bottom))
    pieces = lax.switch(
        comp * 32 + units,
        [atmosphere_route(i) for i in range(32)] + [ocean_route(i) for i in range(32)],
        peer,
    )
    forcing = force(par, pieces, diag, surf, sea_mask)
    f_top, f_bottom = shift_pair(forcing[:HALO], forcing[N - HALO :], "gx")
    own = (field, mix, kappa, sea_mask, top, bottom, forcing, f_top, f_bottom)
    first_columns, last_columns = columns(par, *own)
    before, after = shift_pair(first_columns, last_columns, "gy")
    return sweeps(par, *own, after, before)[None]


def solution(mesh):
    placed = (
        P("comp", None, "gx", "gy"),
        P("comp", "gx", "gy"),
        P("comp", None, "gx", "gy"),
        P("gx", "gy"),
        P("comp", "gx", "gy", None),
        P("comp", "gx", None, "gy", None),
    )
    return jax.shard_map(
        shards, mesh=mesh, in_specs=placed, out_specs=P("comp", None, "gx", "gy"), check_vma=False
    )
```

time: 212 us -> 102 us (0.48)
  the two profiles are of different devices: /device:TPU:3 before, /device:TPU:30 now
where the time goes in v1:
time: 102 us; the launch traced here: 103 us
  starting transfers between devices  45 us (44%)
  Pallas kernels  30.9 us (30%)
  waiting for transfers between devices  17.3 us (17%)
  local copies, waits for them, and re-layouts  6.39 us (6%)
  between operations  2.76 us (3%)
    ppermute x3, starting transfers between devices, shift_pair(): lax.ppermute(low_edge, axis, down)  15.3 us
    pallas_call x1, Pallas kernels, sweeps(): pl.pallas_call(sweep_kernel, in_specs=[SMEM] + [VMEM] * 11, out_specs=VME...  13.9 us
    ppermute x4, starting transfers between devices, routed(): return lax.ppermute(block, BOTH, pairs)  12.3 us
    pallas_call x1, Pallas kernels, band(): pl.pallas_call(band_kernel, grid=(N // step,), in_specs=[pl.BlockSpec((st...  12.2 us
    ppermute x1, starting transfers between devices, shards(): peer = lax.ppermute(surf, BOTH, swap)  9.45 us
    ppermute x3, waiting for transfers between devices, shift_pair(): lax.ppermute(high_edge, axis, up)  8.92 us
    ppermute x4, waiting for transfers between devices, routed(): return lax.ppermute(block, BOTH, pairs)  8.39 us
    ppermute x3, starting transfers between devices, shift_pair(): lax.ppermute(high_edge, axis, up)  7.97 us
  transfers between devices with their start and end apart: 11, of which 4 were waited for; matrix products, arithmetic and copies ran while one was open for 1% of the time, Pallas kernels for 12%

profile of v1, /device:TPU:30, one launch (start us, length us, event | category | flops | bytes accessed | tf_op | source)
XLA Modules:
  0.0 102.6 jit_solution(7816331239646562087)
XLA Ops:
  0.0 1.0 dynamic-slice_bitcast_fusion.surf
  1.0 9.5 %collective-permute-start.224 = (f32[4,128,128]{2,1,0:T(8,128)S(1)}, f32[4,128,128]{2,1,0:T(8,128)S(1)}, u32[]{:S(2)}, u32[]{:S(2)}) collective-permute-start(f32[4,128,128]{2,1,0:T(8,128)S(1)} %dynamic-slice_bitcast_fusion.surf), channel_id=1, source_target_pairs={{0,64},{4,68},{8,72},{12,76},{16,80},{20,84},{24,88},{28,92},{32,9... | collective-permute-start | bytes 786440 | tf_op jit(solution)/shard_map/ppermute | solution.py:428
  10.4 1.3 %slice.297 = s32[1,1,1,1]{1,3,2,0:T(1,128)} slice(s32[1,128,1,2]{1,3,2,0:T(2,128)} %param.74), slice={[0:1], [0:1], [0:1], [0:1]} | slice | bytes 8 | tf_op jit(solution)/shard_map/slice | solution.py:429
  14.3 1.2 %copy-done = f32[1,16,128,128]{3,2,1,0:T(8,128)S(1)} copy-done((f32[1,16,128,128]{3,2,1,0:T(8,128)S(1)}, f32[1,16,128,128]{3,2,1,0:T(8,128)}, u32[]{:S(2)}) %copy-start) | copy-done | bytes 1048600
  15.6 1.2 %copy-done.2 = f32[1,16,128,128]{3,2,1,0:T(8,128)S(1)} copy-done((f32[1,16,128,128]{3,2,1,0:T(8,128)S(1)}, f32[1,16,128,128]{3,2,1,0:T(8,128)}, u32[]{:S(2)}) %copy-start.2) | copy-done | bytes 1048600
  19.0 3.6 %collective-permute-start.225 = (f32[32,8,128]{2,1,0:T(8,128)S(1)}, f32[32,8,128]{2,1,0:T(8,128)S(1)}, u32[]{:S(2)}, u32[]{:S(2)}) collective-permute-start(f32[32,8,128]{2,1,0:T(8,128)S(1)} %get-tuple-element.81), channel_id=1, source_target_pairs={{0,4},{4,8},{8,12},{12,16},{16,20},{20,24},{24,28},{28,32},{32,36}... | collective-permute-start | bytes 393224 | tf_op jit(solution)/shard_map/ppermute | solution.py:375
  22.7 4.3 %collective-permute-start.226 = (f32[32,8,128]{2,1,0:T(8,128)S(1)}, f32[32,8,128]{2,1,0:T(8,128)S(1)}, u32[]{:S(2)}, u32[]{:S(2)}) collective-permute-start(f32[32,8,128]{2,1,0:T(8,128)S(1)} %get-tuple-element.82), channel_id=1, source_target_pairs={{4,0},{8,4},{12,8},{16,12},{20,16},{24,20},{28,24},{32,28},{36,32}... | collective-permute-start | bytes 393224 | tf_op jit(solution)/shard_map/ppermute | solution.py:375
  27.0 12.2 %band.1.diag = f32[4,128,128]{2,1,0:T(8,128)} custom-call(f32[128,2,128,128]{3,2,1,0:T(8,128)} %bitcast.21), custom_call_target="tpu_custom_call" | custom-call | flops 4194304 | bytes 16777216 | tf_op jit(solution)/shard_map/band/pallas_call | solution.py:56
  39.3 20.8 %conditional.1 = (f32[4,128,128]{2,1,0:T(8,128)}, f32[4,128,128]{2,1,0:T(8,128)}, f32[4,64,128]{2,1,0:T(8,128)}, f32[4,64,128]{2,1,0:T(8,128)}) conditional(s32[]{:T(128)} %clamp.3, f32[4,128,128]{2,1,0:T(8,128)S(1)} %collective-permute-done.224, f32[4,128,128]{2,1,0:T(8,128)S(1)} %collective-permute-done.224, ...), branch_computations={%region_0.1_spmd, %region_1.2_spmd, %region_2.3_spmd, %region_3.4_... | conditional | bytes 3408064 | solution.py:435
  39.4 2.1 %collective-permute-start.13 = (f32[4,128,128]{2,1,0:T(8,128)S(1)}, f32[4,128,128]{2,1,0:T(8,128)}, u32[]{:S(2)}, u32[]{:S(2)}) collective-permute-start(f32[4,128,128]{2,1,0:T(8,128)S(1)} %param.35), channel_id=1, source_target_pairs={{76,64},{84,68},{92,72},{100,76},{108,80},{116,84},{124,88},{68,92... | collective-permute-start | bytes 786440 | tf_op jit(solution)/shard_map/cond/branch_35_fun/ppermute | solution.py:387
  41.4 2.9 %collective-permute-start.12 = (f32[4,128,128]{2,1,0:T(8,128)S(1)}, f32[4,128,128]{2,1,0:T(8,128)}, u32[]{:S(2)}, u32[]{:S(2)}) collective-permute-start(f32[4,128,128]{2,1,0:T(8,128)S(1)} %param.35), channel_id=1, source_target_pairs={{72,64},{80,68},{88,72},{96,76},{104,80},{112,84},{120,88},{64,92}... | collective-permute-start | bytes 786440 | tf_op jit(solution)/shard_map/cond/branch_35_fun/ppermute | solution.py:387
  44.4 5.4 %collective-permute-start.15 = (f32[4,64,128]{2,1,0:T(8,128)S(1)}, f32[4,64,128]{2,1,0:T(8,128)}, u32[]{:S(2)}, u32[]{:S(2)}) collective-permute-start(f32[4,64,128]{2,1,0:T(8,128)S(1)} %slice.265), channel_id=1, source_target_pairs={{72,64},{80,68},{88,72},{96,76},{104,80},{112,84},{120,88},{64,92}... | collective-permute-start | bytes 393224 | tf_op jit(solution)/shard_map/cond/branch_35_fun/ppermute | solution.py:387
  49.8 1.9 %collective-permute-start.14 = (f32[4,64,128]{2,1,0:T(8,128)S(1)}, f32[4,64,128]{2,1,0:T(8,128)}, u32[]{:S(2)}, u32[]{:S(2)}) collective-permute-start(f32[4,64,128]{2,1,0:T(8,128)S(1)} %slice.265), channel_id=1, source_target_pairs={{68,64},{76,68},{84,72},{92,76},{100,80},{108,84},{116,88},{124,92... | collective-permute-start | bytes 393224 | tf_op jit(solution)/shard_map/cond/branch_35_fun/ppermute | solution.py:387
  51.7 2.0 %collective-permute-done.15 = f32[4,64,128]{2,1,0:T(8,128)} collective-permute-done((f32[4,64,128]{2,1,0:T(8,128)S(1)}, f32[4,64,128]{2,1,0:T(8,128)}, u32[]{:S(2)}, u32[]{:S(2)}) %collective-permute-start.15) | collective-permute-done | bytes 131104 | tf_op jit(solution)/shard_map/cond/branch_35_fun/ppermute | solution.py:387
  53.7 6.4 %collective-permute-done.14 = f32[4,64,128]{2,1,0:T(8,128)} collective-permute-done((f32[4,64,128]{2,1,0:T(8,128)S(1)}, f32[4,64,128]{2,1,0:T(8,128)}, u32[]{:S(2)}, u32[]{:S(2)}) %collective-permute-start.14) | collective-permute-done | bytes 131104 | tf_op jit(solution)/shard_map/cond/branch_35_fun/ppermute | solution.py:387
  60.2 1.4 %force.1.forcing = f32[128,128]{1,0:T(8,128)S(1)} custom-call(s32[4]{0:T(128)S(1)} %pad_add_fusion.par, f32[4,128,128]{2,1,0:T(8,128)} %get-tuple-element.86.a, f32[4,128,128]{2,1,0:T(8,128)} %get-tuple-element.87.b, f32[4,64,128]{2,1,0:T(8,128)} %get-tuple-element.88.c1, f32[4,64,128]{2,1,0:T(8,128)} %get-tuple-element.89.c2, f32[4,128,128]{2,1,0:T(8,128)S(1)} %copy-done.4, ...), custom_call_target="tpu_custom_call" | custom-call | tf_op jit(solution)/shard_map/force/pallas_call | solution.py:144
  61.5 9.1 %collective-permute-start.228 = (f32[8,128]{1,0:T(8,128)S(1)}, f32[8,128]{1,0:T(8,128)S(1)}, u32[]{:S(2)}, u32[]{:S(2)}) collective-permute-start(f32[8,128]{1,0:T(8,128)S(1)} %get-tuple-element.157), channel_id=1, source_target_pairs={{4,0},{8,4},{12,8},{16,12},{20,16},{24,20},{28,24},{32,28},{36,32}... | collective-permute-start | bytes 12296 | tf_op jit(solution)/shard_map/ppermute | solution.py:375
  70.6 1.9 %collective-permute-start.227 = (f32[8,128]{1,0:T(8,128)S(1)}, f32[8,128]{1,0:T(8,128)S(1)}, u32[]{:S(2)}, u32[]{:S(2)}) collective-permute-start(f32[8,128]{1,0:T(8,128)S(1)} %get-tuple-element.158), channel_id=1, source_target_pairs={{0,4},{4,8},{8,12},{12,16},{16,20},{20,24},{24,28},{28,32},{32,36}... | collective-permute-start | bytes 12296 | tf_op jit(solution)/shard_map/ppermute | solution.py:375
  72.5 5.7 %collective-permute-done.227.f_top = f32[8,128]{1,0:T(8,128)S(1)} collective-permute-done((f32[8,128]{1,0:T(8,128)S(1)}, f32[8,128]{1,0:T(8,128)S(1)}, u32[]{:S(2)}, u32[]{:S(2)}) %collective-permute-start.227) | collective-permute-done | bytes 4128 | tf_op jit(solution)/shard_map/ppermute | solution.py:375
  78.2 2.9 %columns.1 = (f32[144,128]{1,0:T(8,128)S(1)}, f32[144,128]{1,0:T(8,128)S(1)}) custom-call(s32[4]{0:T(128)S(1)} %pad_add_fusion.par, f32[16,128,128]{2,1,0:T(8,128)S(1)} %bitcast.13, f32[16,128,128]{2,1,0:T(8,128)S(1)} %bitcast.16, f32[128,128]{1,0:T(8,128)S(1)} %bitcast.19, s32[128,128]{1,0:T(8,128)S(1)} %copy-done.6, ...), custom_call_target="tpu_custom_call" | custom-call | tf_op jit(solution)/shard_map/columns/pallas_call | solution.py:200
  81.2 1.9 %collective-permute-start.229 = (f32[144,128]{1,0:T(8,128)S(1)}, f32[144,128]{1,0:T(8,128)S(1)}, u32[]{:S(2)}, u32[]{:S(2)}) collective-permute-start(f32[144,128]{1,0:T(8,128)S(1)} %get-tuple-element.91), channel_id=1, source_target_pairs={{1,0},{2,1},{3,2},{5,4},{6,5},{7,6},{9,8},{10,9},{11,10},{13,12},{... | collective-permute-start | bytes 221192 | tf_op jit(solution)/shard_map/ppermute | solution.py:375
  83.1 2.4 %collective-permute-start.230 = (f32[144,128]{1,0:T(8,128)S(1)}, f32[144,128]{1,0:T(8,128)S(1)}, u32[]{:S(2)}, u32[]{:S(2)}) collective-permute-start(f32[144,128]{1,0:T(8,128)S(1)} %get-tuple-element.92), channel_id=1, source_target_pairs={{0,1},{1,2},{2,3},{4,5},{5,6},{6,7},{8,9},{9,10},{10,11},{12,13},{... | collective-permute-start | bytes 221192 | tf_op jit(solution)/shard_map/ppermute | solution.py:375
  85.5 3.2 %collective-permute-done.230.right = f32[144,128]{1,0:T(8,128)S(1)} collective-permute-done((f32[144,128]{1,0:T(8,128)S(1)}, f32[144,128]{1,0:T(8,128)S(1)}, u32[]{:S(2)}, u32[]{:S(2)}) %collective-permute-start.230) | collective-permute-done | bytes 73760 | tf_op jit(solution)/shard_map/ppermute | solution.py:375
  88.8 13.9 %sweeps.1 = f32[16,128,128]{2,1,0:T(8,128)} custom-call(s32[4]{0:T(128)S(1)} %pad_add_fusion.par, f32[16,128,128]{2,1,0:T(8,128)S(1)} %bitcast.14, f32[16,128,128]{2,1,0:T(8,128)S(1)} %bitcast.17, f32[128,128]{1,0:T(8,128)S(1)} %bitcast.20, s32[128,128]{1,0:T(8,128)S(1)} %copy-done.6, f32[32,8,128]{2,1,0:T(8,128)S(1)} %collective-permute-done.225.top, ...), custom_call_target="tpu_custom_call" | custom-call | tf_op jit(solution)/shard_map/sweeps/pallas_call | solution.py:360
  (27 shorter events, 2.4 us)
Async XLA Ops:
  1.0 38.3 %collective-permute-start.224 = (f32[4,128,128]{2,1,0:T(8,128)S(1)}, f32[4,128,128]{2,1,0:T(8,128)S(1)}, u32[]{:S(2)}, u32[]{:S(2)}) collective-permute-start(f32[4,128,128]{2,1,0:T(8,128)S(1)} %dynamic-slice_bitcast_fusion.surf), channel_id=1, source_target_pairs={{0,64},{4,68},{8,72},{12,76},{16,80},{20,84},{24,88},{28,92},{32,9... | collective-permute-start | bytes 786440 | tf_op jit(solution)/shard_map/ppermute | solution.py:428
  14.3 1.2 %copy-start = (f32[1,16,128,128]{3,2,1,0:T(8,128)S(1)}, f32[1,16,128,128]{3,2,1,0:T(8,128)}, u32[]{:S(2)}) copy-start(f32[1,16,128,128]{3,2,1,0:T(8,128)} %param.70) | copy-start | bytes 3145732
  15.6 1.2 %copy-start.2 = (f32[1,16,128,128]{3,2,1,0:T(8,128)S(1)}, f32[1,16,128,128]{3,2,1,0:T(8,128)}, u32[]{:S(2)}) copy-start(f32[1,16,128,128]{3,2,1,0:T(8,128)} %param.72) | copy-start | bytes 3145732
  16.8 0.8 copy-start.5
  17.6 0.8 copy-start.7
  19.0 20.2 %collective-permute-start.225 = (f32[32,8,128]{2,1,0:T(8,128)S(1)}, f32[32,8,128]{2,1,0:T(8,128)S(1)}, u32[]{:S(2)}, u32[]{:S(2)}) collective-permute-start(f32[32,8,128]{2,1,0:T(8,128)S(1)} %get-tuple-element.81), channel_id=1, source_target_pairs={{0,4},{4,8},{8,12},{12,16},{16,20},{20,24},{24,28},{28,32},{32,36}... | collective-permute-start | bytes 393224 | tf_op jit(solution)/shard_map/ppermute | solution.py:375
  22.7 16.6 %collective-permute-start.226 = (f32[32,8,128]{2,1,0:T(8,128)S(1)}, f32[32,8,128]{2,1,0:T(8,128)S(1)}, u32[]{:S(2)}, u32[]{:S(2)}) collective-permute-start(f32[32,8,128]{2,1,0:T(8,128)S(1)} %get-tuple-element.82), channel_id=1, source_target_pairs={{4,0},{8,4},{12,8},{16,12},{20,16},{24,20},{28,24},{32,28},{36,32}... | collective-permute-start | bytes 393224 | tf_op jit(solution)/shard_map/ppermute | solution.py:375
  39.3 20.9 %copy-start.4 = (f32[4,128,128]{2,1,0:T(8,128)S(1)}, f32[4,128,128]{2,1,0:T(8,128)}, u32[]{:S(2)}) copy-start(f32[4,128,128]{2,1,0:T(8,128)} %band.1.diag) | copy-start | bytes 786436
  39.3 20.9 %copy-start.6 = (s32[128,128]{1,0:T(8,128)S(1)}, s32[128,128]{1,0:T(8,128)}, u32[]{:S(2)}) copy-start(s32[128,128]{1,0:T(8,128)} %mask.7) | copy-start | bytes 196612
  39.3 39.0 %copy-start.1 = (f32[1,16,128,128]{3,2,1,0:T(8,128)S(1)}, f32[1,16,128,128]{3,2,1,0:T(8,128)}, u32[]{:S(2)}) copy-start(f32[1,16,128,128]{3,2,1,0:T(8,128)} %param.70) | copy-start | bytes 3145732
  39.3 39.0 %copy-start.3 = (f32[1,16,128,128]{3,2,1,0:T(8,128)S(1)}, f32[1,16,128,128]{3,2,1,0:T(8,128)}, u32[]{:S(2)}) copy-start(f32[1,16,128,128]{3,2,1,0:T(8,128)} %param.72) | copy-start | bytes 3145732
  39.3 39.0 %copy-start.8 = (f32[1,128,128]{2,1,0:T(8,128)S(1)}, f32[1,128,128]{2,1,0:T(8,128)}, u32[]{:S(2)}) copy-start(f32[1,128,128]{2,1,0:T(8,128)} %param.71) | copy-start | bytes 196612
  39.4 20.8 %collective-permute-start.13 = (f32[4,128,128]{2,1,0:T(8,128)S(1)}, f32[4,128,128]{2,1,0:T(8,128)}, u32[]{:S(2)}, u32[]{:S(2)}) collective-permute-start(f32[4,128,128]{2,1,0:T(8,128)S(1)} %param.35), channel_id=1, source_target_pairs={{76,64},{84,68},{92,72},{100,76},{108,80},{116,84},{124,88},{68,92... | collective-permute-start | bytes 786440 | tf_op jit(solution)/shard_map/cond/branch_35_fun/ppermute | solution.py:387
  41.4 18.7 %collective-permute-start.12 = (f32[4,128,128]{2,1,0:T(8,128)S(1)}, f32[4,128,128]{2,1,0:T(8,128)}, u32[]{:S(2)}, u32[]{:S(2)}) collective-permute-start(f32[4,128,128]{2,1,0:T(8,128)S(1)} %param.35), channel_id=1, source_target_pairs={{72,64},{80,68},{88,72},{96,76},{104,80},{112,84},{120,88},{64,92}... | collective-permute-start | bytes 786440 | tf_op jit(solution)/shard_map/cond/branch_35_fun/ppermute | solution.py:387
  44.4 9.3 %collective-permute-start.15 = (f32[4,64,128]{2,1,0:T(8,128)S(1)}, f32[4,64,128]{2,1,0:T(8,128)}, u32[]{:S(2)}, u32[]{:S(2)}) collective-permute-start(f32[4,64,128]{2,1,0:T(8,128)S(1)} %slice.265), channel_id=1, source_target_pairs={{72,64},{80,68},{88,72},{96,76},{104,80},{112,84},{120,88},{64,92}... | collective-permute-start | bytes 393224 | tf_op jit(solution)/shard_map/cond/branch_35_fun/ppermute | solution.py:387
  49.8 10.3 %collective-permute-start.14 = (f32[4,64,128]{2,1,0:T(8,128)S(1)}, f32[4,64,128]{2,1,0:T(8,128)}, u32[]{:S(2)}, u32[]{:S(2)}) collective-permute-start(f32[4,64,128]{2,1,0:T(8,128)S(1)} %slice.265), channel_id=1, source_target_pairs={{68,64},{76,68},{84,72},{92,76},{100,80},{108,84},{116,88},{124,92... | collective-permute-start | bytes 393224 | tf_op jit(solution)/shard_map/cond/branch_35_fun/ppermute | solution.py:387
  61.5 11.0 %collective-permute-start.228 = (f32[8,128]{1,0:T(8,128)S(1)}, f32[8,128]{1,0:T(8,128)S(1)}, u32[]{:S(2)}, u32[]{:S(2)}) collective-permute-start(f32[8,128]{1,0:T(8,128)S(1)} %get-tuple-element.157), channel_id=1, source_target_pairs={{4,0},{8,4},{12,8},{16,12},{20,16},{24,20},{28,24},{32,28},{36,32}... | collective-permute-start | bytes 12296 | tf_op jit(solution)/shard_map/ppermute | solution.py:375
  70.6 7.6 %collective-permute-start.227 = (f32[8,128]{1,0:T(8,128)S(1)}, f32[8,128]{1,0:T(8,128)S(1)}, u32[]{:S(2)}, u32[]{:S(2)}) collective-permute-start(f32[8,128]{1,0:T(8,128)S(1)} %get-tuple-element.158), channel_id=1, source_target_pairs={{0,4},{4,8},{8,12},{12,16},{16,20},{20,24},{24,28},{28,32},{32,36}... | collective-permute-start | bytes 12296 | tf_op jit(solution)/shard_map/ppermute | solution.py:375
  81.2 4.3 %collective-permute-start.229 = (f32[144,128]{1,0:T(8,128)S(1)}, f32[144,128]{1,0:T(8,128)S(1)}, u32[]{:S(2)}, u32[]{:S(2)}) collective-permute-start(f32[144,128]{1,0:T(8,128)S(1)} %get-tuple-element.91), channel_id=1, source_target_pairs={{1,0},{2,1},{3,2},{5,4},{6,5},{7,6},{9,8},{10,9},{11,10},{13,12},{... | collective-permute-start | bytes 221192 | tf_op jit(solution)/shard_map/ppermute | solution.py:375
  83.1 5.7 %collective-permute-start.230 = (f32[144,128]{1,0:T(8,128)S(1)}, f32[144,128]{1,0:T(8,128)S(1)}, u32[]{:S(2)}, u32[]{:S(2)}) collective-permute-start(f32[144,128]{1,0:T(8,128)S(1)} %get-tuple-element.92), channel_id=1, source_target_pairs={{0,1},{1,2},{2,3},{4,5},{5,6},{6,7},{8,9},{9,10},{10,11},{12,13},{... | collective-permute-start | bytes 221192 | tf_op jit(solution)/shard_map/ppermute | solution.py:375

commit v2 on v1

--- a/solution.py
+++ b/solution.py
@@ -33,60 +33,113 @@
     return pltpu.CompilerParams(vmem_limit_bytes=vmem_mib * 2**20)
 
 
-def band_kernel(w_ref, out_ref):
-    rows = w_ref.shape[0]
+CHUNKS = 16
+
+
+def band_kernel(w_hbm, out_ref, w_ref, sems):
+    rows = N // CHUNKS
+
+    def copy(i):
+        at = pl.ds(i * rows, rows)
+        return pltpu.make_async_copy(w_hbm.at[at], w_ref.at[at], sems.at[i])
+
+    for i in range(CHUNKS):
+        copy(i).start()
     sub = lax.broadcasted_iota(jnp.int32, (8, N), 0)
     lane = lax.broadcasted_iota(jnp.int32, (8, N), 1)
     same = sub == lane % 8
     after = sub == (lane + 7) % 8
-    for k in range(2):
-        own, nxt = [], []
-        for x in range(rows):
-            tile = w_ref[x, k, 0:8, :]
-            for i in range(1, N // 8):
-                tile = tile + w_ref[x, k, 8 * i : 8 * i + 8, :]
-            own.append(jnp.sum(jnp.where(same, tile, 0.0), axis=0, keepdims=True))
-            nxt.append(jnp.sum(jnp.where(after, tile, 0.0), axis=0, keepdims=True))
-        out_ref[k] = jnp.concatenate(own, axis=0)
-        out_ref[2 + k] = jnp.concatenate(nxt, axis=0)
+
+    def body(i, carry):
+        copy(i).wait()
+        base = pl.multiple_of(i * rows, rows)
+        for k in range(2):
+            own, nxt = [], []
+            for x in range(rows):
+                tile = w_ref[base + x, k, 0:8, :]
+                for t in range(1, N // 8):
+                    tile = tile + w_ref[base + x, k, 8 * t : 8 * t + 8, :]
+                own.append(jnp.sum(jnp.where(same, tile, 0.0), axis=0, keepdims=True))
+                nxt.append(jnp.sum(jnp.where(after, tile, 0.0), axis=0, keepdims=True))
+            out_ref[k, pl.ds(base, rows)] = jnp.concatenate(own, axis=0)
+            out_ref[2 + k, pl.ds(base, rows)] = jnp.concatenate(nxt, axis=0)
+        return carry
+
+    lax.fori_loop(0, CHUNKS, body, 0)
 
 
 def band(weight):
-    step = 8
     return pl.pallas_call(
         band_kernel,
-        grid=(N // step,),
-        in_specs=[pl.BlockSpec((step, 2, N, N), lambda i: (i, 0, 0, 0))],
-        out_specs=pl.BlockSpec((4, step, N), lambda i: (0, i, 0)),
+        in_specs=[pl.BlockSpec(memory_space=pl.ANY)],
+        out_specs=VMEM,
         out_shape=jax.ShapeDtypeStruct((4, N, N), f32),
-        compiler_params=params(56),
+        scratch_shapes=[pltpu.VMEM((N, 2, N, N), f32), pltpu.SemaphoreType.DMA((CHUNKS,))],
+        compiler_params=params(48),
         cost_estimate=pl.CostEstimate(flops=2**22, bytes_accessed=2**24, transcendentals=0),
         name="band",
     )(weight)
 
 
-def edge_kernel(par, state, mixing, kappa, mask, top, bottom):
-    ocean = par[0] == 1
-    for out, low in ((top, 0), (bottom, N - HALO)):
-        rows = slice(low, low + HALO)
-        sea = jnp.where(ocean, mask[rows].astype(f32), 1.0)
+def edge_kernel(
+    where, source, state, mixing, kappa, mask, top, bottom, par, choice, s_ref, m_ref, k_ref, i_ref, sems
+):
+    comp, x = where[0], where[1]
+    copies = []
+    for side, low in enumerate((0, N - HALO)):
+        rows = pl.ds(low, HALO)
+        for n, (src, dst) in enumerate(
+            (
+                (state.at[:, rows], s_ref.at[side]),
+                (mixing.at[:, rows], m_ref.at[side]),
+                (kappa.at[rows], k_ref.at[side]),
+                (mask.at[rows], i_ref.at[side]),
+            )
+        ):
+            copies.append(pltpu.make_async_copy(src, dst, sems.at[4 * side + n]))
+    for c in copies:
+        c.start()
+    first = source[0, 0]
+    units = lax.rem(first // UNIT + 128 - jnp.where(comp == 1, 4, 1) * x, 32)
+    par[0] = comp
+    par[1] = x
+    par[2] = lax.rem(first, UNIT)
+    par[3] = units
+    choice[0] = comp * 32 + units
+    for c in copies:
+        c.wait()
+    for side, out in enumerate((top, bottom)):
+        sea = jnp.where(comp == 1, i_ref[side].astype(f32), 1.0)
         for level in range(LEV):
-            out[level] = state[level, rows]
+            out[level] = s_ref[side, level]
         for level in range(LEV - 1):
-            out[LEV + level] = mixing[level, rows] * sea
-        out[2 * LEV - 1] = kappa[rows] * sea
-
-
-def edges(par, state, mixing, kappa, mask):
+            out[LEV + level] = m_ref[side, level] * sea
+        out[2 * LEV - 1] = k_ref[side] * sea
+
+
+def edges(where, source, state, mixing, kappa, mask):
     shape = jax.ShapeDtypeStruct((2 * LEV, HALO, N), f32)
+    hbm = pl.BlockSpec(memory_space=pl.ANY)
     return pl.pallas_call(
         edge_kernel,
-        in_specs=[SMEM] + [VMEM] * 4,
-        out_specs=[VMEM, VMEM],
-        out_shape=[shape, shape],
-        compiler_params=params(16),
+        in_specs=[SMEM, SMEM] + [hbm] * 4,
+        out_specs=[VMEM, VMEM, SMEM, SMEM],
+        out_shape=[
+            shape,
+            shape,
+            jax.ShapeDtypeStruct((4,), jnp.int32),
+            jax.ShapeDtypeStruct((1,), jnp.int32),
+        ],
+        scratch_shapes=[
+            pltpu.VMEM((2, LEV, HALO, N), f32),
+            pltpu.VMEM((2, LEV, HALO, N), f32),
+            pltpu.VMEM((2, HALO, N), f32),
+            pltpu.VMEM((2, HALO, N), jnp.int32),
+            pltpu.SemaphoreType.DMA((8,)),
+        ],
+        compiler_params=params(60),
         name="edges",
-    )(par, state, mixing, kappa, mask)
+    )(where, source, state, mixing, kappa, mask)
 
 
 def force_kernel(par, a, b, c1, c2, diag, surf, mask, out, window, rows):
@@ -378,13 +431,29 @@
 BOTH = ("comp", "gx")
 
 
-def routed(block, route):
-    route = route % 32
-    pairs = [
+MERGED = 16
+
+
+def ocean_pairs(route):
+    return [
         (GX + (2 * x + route % GX + ((x >= 8) != (route >= GX))) % GX, GX + x) for x in range(GX)
     ]
-    pairs += [((x + route) // 2 % GX, x) for x in range(GX) if (x + route) % 2 == 0]
+
+
+def atmosphere_pairs(route):
+    return [((x + route) // 2 % GX, x) for x in range(GX) if (x + route) % 2 == 0]
+
+
+def listed(block, entry):
+    pairs = ocean_pairs((entry + 15) % 32) + atmosphere_pairs(entry)
+    if entry == MERGED + 15:
+        pairs += atmosphere_pairs(MERGED)
     return lax.ppermute(block, BOTH, pairs)
+
+
+def atmosphere_routed(block, route):
+    route = route % 32
+    return listed(block, route if route != MERGED else MERGED + 15)
 
 
 def ocean_route(units):
@@ -395,12 +464,26 @@
         whole = (base + odd) % GX
         part = (base + 1 - odd) % GX
         half = peer[:, UNIT:] if odd else peer[:, :UNIT]
-        return (
-            routed(peer, whole),
-            routed(peer, GX + whole),
-            routed(half, part),
-            routed(half, GX + part),
-        )
+        jobs = [(peer, whole), (peer, GX + whole), (half, part), (half, GX + part)]
+        entries = [(route + 17) % 32 for _, route in jobs]
+        if MERGED not in entries:
+            return tuple(listed(block, entry) for (block, _), entry in zip(jobs, entries))
+        results = []
+        last = peer[:1, :8]
+
+        def chained(block, entry):
+            nonlocal last
+            block, _ = lax.optimization_barrier((block, last))
+            last = listed(block, entry)
+            return last
+
+        for (block, _), entry in zip(jobs, entries):
+            if entry != MERGED:
+                results.append(chained(block, entry))
+            else:
+                low, high = chained(block, 17), chained(block, 31)
+                results.append(jnp.where(lax.axis_index("gx") < 8, low, high))
+        return tuple(results)
 
     return run
 
@@ -408,10 +491,10 @@
 def atmosphere_route(units):
     def run(peer):
         return (
-            routed(peer, units),
+            atmosphere_routed(peer, units),
             peer,
-            routed(peer[:, UNIT:], units - 1),
-            routed(peer[:, :UNIT], units + 1),
+            atmosphere_routed(peer[:, UNIT:], units - 1),
+            atmosphere_routed(peer[:, :UNIT], units + 1),
         )
 
     return run
@@ -426,14 +509,14 @@
     surf = lax.dynamic_slice(field, ((LEV - F) * (1 - comp), 0, 0), (F, N, N))
     swap = [(x, GX + x) for x in range(GX)] + [(GX + x, x) for x in range(GX)]
     peer = lax.ppermute(surf, BOTH, swap)
-    first = source_row[0, 0, 0, 0]
-    units = jnp.where(comp == 1, first // UNIT - 4 * gx, first // UNIT - gx) % 32
-    par = jnp.stack([comp, gx, first % UNIT, units]).astype(jnp.int32)
+    where = jnp.stack([comp, gx]).astype(jnp.int32)
+    source = jnp.transpose(source_row[0, :, 0, :])
+    low, high, par, choice = edges(where, source, field, mix, kappa, sea_mask)
     diag = band(regrid_weight[0])
-    top, bottom = shift_pair(*edges(par, field, mix, kappa, sea_mask), "gx")
+    top, bottom = shift_pair(low, high, "gx")
     peer, diag, top, bottom = lax.optimization_barrier((peer, diag, top, bottom))
     pieces = lax.switch(
-        comp * 32 + units,
+        choice[0],
         [atmosphere_route(i) for i in range(32)] + [ocean_route(i) for i in range(32)],
         peer,
     )

time: 102 us -> 82.9 us (0.81)
  starting transfers between devices: 45 us -> 37.4 us
  local copies, waits for them, and re-layouts: 6.39 us -> 1.01 us
  Pallas kernels: 30.9 us -> 26.7 us
  between operations: 2.76 us -> 0.75 us
    ppermute x1, starting transfers between devices: 9.45 us -> 1.31 us  [shards(): peer = lax.ppermute(surf, BOTH, swap)]
    pallas_call x2, Pallas kernels: 12.8 us -> 8.47 us  [the longest x1 6.01 us: band(): pl.pallas_call(band_kernel, in_specs=[pl.BlockSpec(memory_space=pl.ANY)],...]
    unnamed x18 -> x10, local copies, waits for them, and re-layouts: 4.15 us -> 0.03 us
    slice x1 -> x0, local copies, waits for them, and re-layouts: 1.26 us -> none  [shards(): first = source_row[0, 0, 0, 0]]
  transfers between devices with their start and end apart: 11 -> 11, of which waited for: 4 -> 4; matrix products, arithmetic and copies ran while one was open for 1% -> 1% of each run, Pallas kernels for 12% -> 10%
where the time goes in v2:
time: 82.9 us; the launch traced here: 83.3 us
  starting transfers between devices  37.4 us (45%)
  Pallas kernels  26.7 us (32%)
  waiting for transfers between devices  16.7 us (20%)
  local copies, waits for them, and re-layouts  1.01 us (1%)
    ppermute x3, starting transfers between devices, shift_pair(): lax.ppermute(low_edge, axis, down)  15.3 us
    pallas_call x1, Pallas kernels, sweeps(): pl.pallas_call(sweep_kernel, in_specs=[SMEM] + [VMEM] * 11, out_specs=VME...  13.9 us
    ppermute x4, starting transfers between devices, listed(): return lax.ppermute(block, BOTH, pairs)  12.7 us
    ppermute x3, waiting for transfers between devices, shift_pair(): lax.ppermute(high_edge, axis, up)  8.92 us
    ppermute x3, starting transfers between devices, shift_pair(): lax.ppermute(high_edge, axis, up)  8.15 us
    ppermute x4, waiting for transfers between devices, listed(): return lax.ppermute(block, BOTH, pairs)  7.74 us
    pallas_call x1, Pallas kernels, band(): pl.pallas_call(band_kernel, in_specs=[pl.BlockSpec(memory_space=pl.ANY)],...  6.01 us
    pallas_call x1, Pallas kernels, columns(): pl.pallas_call(column_kernel, in_specs=[SMEM] + [VMEM] * 9, out_specs=[VM...  2.93 us
  transfers between devices with their start and end apart: 11, of which 4 were waited for; matrix products, arithmetic and copies ran while one was open for 1% of the time, Pallas kernels for 10%

profile of v2, /device:TPU:30, one launch (start us, length us, event | category | flops | bytes accessed | tf_op | source)
XLA Modules:
  0.0 83.3 jit_solution(15941120085236520960)
XLA Ops:
  0.0 1.0 %dynamic-slice_bitcast_fusion.surf = f32[4,128,128]{2,1,0:T(8,128)S(1)} fusion(f32[1,16,128,128]{3,2,1,0:T(8,128)} %param.70, s32[]{:T(128)S(6)} %select_n.31), kind=kLoop, calls=%fused_computation.4 | loop fusion | bytes 524292 | tf_op jit(solution)/shard_map/dynamic_slice | solution.py:509
  1.0 1.3 %collective-permute-start.228 = (f32[4,128,128]{2,1,0:T(8,128)S(1)}, f32[4,128,128]{2,1,0:T(8,128)S(1)}, u32[]{:S(2)}, u32[]{:S(2)}) collective-permute-start(f32[4,128,128]{2,1,0:T(8,128)S(1)} %dynamic-slice_bitcast_fusion.surf), channel_id=1, source_target_pairs={{0,64},{4,68},{8,72},{12,76},{16,80},{20,84},{24,88},{28,92},{32,9... | collective-permute-start | bytes 786440 | tf_op jit(solution)/shard_map/ppermute | solution.py:511
  2.3 0.7 pad_add_fusion.where
  2.9 2.5 %edges.1 = (f32[32,8,128]{2,1,0:T(8,128)}, f32[32,8,128]{2,1,0:T(8,128)}, s32[4]{0:T(128)}, s32[1]{0:T(128)}) custom-call(s32[2]{0:T(128)} %pad_add_fusion.where, s32[2,128]{1,0:T(2,128)} %bitcast.23, f32[16,128,128]{2,1,0:T(8,128)} %bitcast.13, f32[16,128,128]{2,1,0:T(8,128)} %bitcast.16, f32[128,128]{1,0:T(8,128)} %bitcast.19, s32[128,128]{1,0:T(8,128)} %mask.7), custom_call_target="tpu_custom_call" | custom-call | tf_op jit(solution)/shard_map/edges/pallas_call | solution.py:123
  5.4 3.8 %collective-permute-start.229 = (f32[32,8,128]{2,1,0:T(8,128)}, f32[32,8,128]{2,1,0:T(8,128)S(1)}, u32[]{:S(2)}, u32[]{:S(2)}) collective-permute-start(f32[32,8,128]{2,1,0:T(8,128)} %get-tuple-element.100), channel_id=1, source_target_pairs={{0,4},{4,8},{8,12},{12,16},{16,20},{20,24},{24,28},{28,32},{32,36}... | collective-permute-start | bytes 393224 | tf_op jit(solution)/shard_map/ppermute | solution.py:428
  9.2 4.3 %collective-permute-start.230 = (f32[32,8,128]{2,1,0:T(8,128)}, f32[32,8,128]{2,1,0:T(8,128)S(1)}, u32[]{:S(2)}, u32[]{:S(2)}) collective-permute-start(f32[32,8,128]{2,1,0:T(8,128)} %get-tuple-element.101), channel_id=1, source_target_pairs={{4,0},{8,4},{12,8},{16,12},{20,16},{24,20},{28,24},{32,28},{36,32}... | collective-permute-start | bytes 393224 | tf_op jit(solution)/shard_map/ppermute | solution.py:428
  14.1 6.0 %band.1.diag = f32[4,128,128]{2,1,0:T(8,128)S(1)} custom-call(f32[128,2,128,128]{3,2,1,0:T(8,128)} %bitcast.22), custom_call_target="tpu_custom_call" | custom-call | flops 4194304 | bytes 16777216 | tf_op jit(solution)/shard_map/band/pallas_call | solution.py:72
  20.2 0.0 copy-start.2
  20.2 20.5 %conditional.1 = (f32[4,128,128]{2,1,0:T(8,128)}, f32[4,128,128]{2,1,0:T(8,128)}, f32[4,64,128]{2,1,0:T(8,128)}, f32[4,64,128]{2,1,0:T(8,128)}) conditional(s32[]{:T(128)} %bitcast.9, f32[4,128,128]{2,1,0:T(8,128)S(1)} %collective-permute-done.228, f32[4,128,128]{2,1,0:T(8,128)S(1)} %collective-permute-done.228, ...), branch_computations={%region_0.0_spmd, %region_1.0_spmd, %region_2.0_spmd, %region_3.0_... | conditional | flops 65540 | bytes 6291758 | solution.py:518
  20.3 2.1 %collective-permute-start.13 = (f32[4,128,128]{2,1,0:T(8,128)S(1)}, f32[4,128,128]{2,1,0:T(8,128)}, u32[]{:S(2)}, u32[]{:S(2)}) collective-permute-start(f32[4,128,128]{2,1,0:T(8,128)S(1)} %param.35), channel_id=1, source_target_pairs={{76,64},{84,68},{92,72},{100,76},{108,80},{116,84},{124,88},{68,92... | collective-permute-start | bytes 786440 | tf_op jit(solution)/shard_map/cond/branch_35_fun/ppermute | solution.py:451
  22.3 2.9 %collective-permute-start.12 = (f32[4,128,128]{2,1,0:T(8,128)S(1)}, f32[4,128,128]{2,1,0:T(8,128)}, u32[]{:S(2)}, u32[]{:S(2)}) collective-permute-start(f32[4,128,128]{2,1,0:T(8,128)S(1)} %param.35), channel_id=1, source_target_pairs={{72,64},{80,68},{88,72},{96,76},{104,80},{112,84},{120,88},{64,92}... | collective-permute-start | bytes 786440 | tf_op jit(solution)/shard_map/cond/branch_35_fun/ppermute | solution.py:451
  25.3 5.8 %collective-permute-start.15 = (f32[4,64,128]{2,1,0:T(8,128)S(1)}, f32[4,64,128]{2,1,0:T(8,128)}, u32[]{:S(2)}, u32[]{:S(2)}) collective-permute-start(f32[4,64,128]{2,1,0:T(8,128)S(1)} %slice.267), channel_id=1, source_target_pairs={{72,64},{80,68},{88,72},{96,76},{104,80},{112,84},{120,88},{64,92}... | collective-permute-start | bytes 393224 | tf_op jit(solution)/shard_map/cond/branch_35_fun/ppermute | solution.py:451
  31.1 1.9 %collective-permute-start.14 = (f32[4,64,128]{2,1,0:T(8,128)S(1)}, f32[4,64,128]{2,1,0:T(8,128)}, u32[]{:S(2)}, u32[]{:S(2)}) collective-permute-start(f32[4,64,128]{2,1,0:T(8,128)S(1)} %slice.267), channel_id=1, source_target_pairs={{68,64},{76,68},{84,72},{92,76},{100,80},{108,84},{116,88},{124,92... | collective-permute-start | bytes 393224 | tf_op jit(solution)/shard_map/cond/branch_35_fun/ppermute | solution.py:451
  33.0 3.5 %collective-permute-done.15 = f32[4,64,128]{2,1,0:T(8,128)} collective-permute-done((f32[4,64,128]{2,1,0:T(8,128)S(1)}, f32[4,64,128]{2,1,0:T(8,128)}, u32[]{:S(2)}, u32[]{:S(2)}) %collective-permute-start.15) | collective-permute-done | bytes 131104 | tf_op jit(solution)/shard_map/cond/branch_35_fun/ppermute | solution.py:451
  36.5 4.2 %collective-permute-done.14 = f32[4,64,128]{2,1,0:T(8,128)} collective-permute-done((f32[4,64,128]{2,1,0:T(8,128)S(1)}, f32[4,64,128]{2,1,0:T(8,128)}, u32[]{:S(2)}, u32[]{:S(2)}) %collective-permute-start.14) | collective-permute-done | bytes 131104 | tf_op jit(solution)/shard_map/cond/branch_35_fun/ppermute | solution.py:451
  40.8 1.4 %force.1.forcing = f32[128,128]{1,0:T(8,128)S(1)} custom-call(s32[4]{0:T(128)S(1)} %copy-done.4, f32[4,128,128]{2,1,0:T(8,128)} %get-tuple-element.106.a, f32[4,128,128]{2,1,0:T(8,128)} %get-tuple-element.107.b, f32[4,64,128]{2,1,0:T(8,128)} %get-tuple-element.108.c1, f32[4,64,128]{2,1,0:T(8,128)} %get-tuple-element.109.c2, f32[4,128,128]{2,1,0:T(8,128)S(1)} %band.1.diag, ...), custom_call_target="tpu_custom_call" | custom-call | tf_op jit(solution)/shard_map/force/pallas_call | solution.py:197
  42.1 9.1 %collective-permute-start.232 = (f32[8,128]{1,0:T(8,128)S(1)}, f32[8,128]{1,0:T(8,128)S(1)}, u32[]{:S(2)}, u32[]{:S(2)}) collective-permute-start(f32[8,128]{1,0:T(8,128)S(1)} %get-tuple-element.177), channel_id=1, source_target_pairs={{4,0},{8,4},{12,8},{16,12},{20,16},{24,20},{28,24},{32,28},{36,32}... | collective-permute-start | bytes 12296 | tf_op jit(solution)/shard_map/ppermute | solution.py:428
  51.2 1.9 %collective-permute-start.231 = (f32[8,128]{1,0:T(8,128)S(1)}, f32[8,128]{1,0:T(8,128)S(1)}, u32[]{:S(2)}, u32[]{:S(2)}) collective-permute-start(f32[8,128]{1,0:T(8,128)S(1)} %get-tuple-element.178), channel_id=1, source_target_pairs={{0,4},{4,8},{8,12},{12,16},{16,20},{20,24},{24,28},{28,32},{32,36}... | collective-permute-start | bytes 12296 | tf_op jit(solution)/shard_map/ppermute | solution.py:428
  53.2 5.7 %collective-permute-done.231.f_top = f32[8,128]{1,0:T(8,128)S(1)} collective-permute-done((f32[8,128]{1,0:T(8,128)S(1)}, f32[8,128]{1,0:T(8,128)S(1)}, u32[]{:S(2)}, u32[]{:S(2)}) %collective-permute-start.231) | collective-permute-done | bytes 4128 | tf_op jit(solution)/shard_map/ppermute | solution.py:428
  58.8 2.9 %columns.1 = (f32[144,128]{1,0:T(8,128)S(1)}, f32[144,128]{1,0:T(8,128)S(1)}) custom-call(s32[4]{0:T(128)S(1)} %copy-done.4, f32[16,128,128]{2,1,0:T(8,128)S(1)} %bitcast.14, f32[16,128,128]{2,1,0:T(8,128)S(1)} %bitcast.17, f32[128,128]{1,0:T(8,128)S(1)} %bitcast.20, s32[128,128]{1,0:T(8,128)S(1)} %copy-done.2, ...), custom_call_target="tpu_custom_call" | custom-call | tf_op jit(solution)/shard_map/columns/pallas_call | solution.py:253
  61.8 1.9 %collective-permute-start.233 = (f32[144,128]{1,0:T(8,128)S(1)}, f32[144,128]{1,0:T(8,128)S(1)}, u32[]{:S(2)}, u32[]{:S(2)}) collective-permute-start(f32[144,128]{1,0:T(8,128)S(1)} %get-tuple-element.111), channel_id=1, source_target_pairs={{1,0},{2,1},{3,2},{5,4},{6,5},{7,6},{9,8},{10,9},{11,10},{13,12},{... | collective-permute-start | bytes 221192 | tf_op jit(solution)/shard_map/ppermute | solution.py:428
  63.7 2.4 %collective-permute-start.234 = (f32[144,128]{1,0:T(8,128)S(1)}, f32[144,128]{1,0:T(8,128)S(1)}, u32[]{:S(2)}, u32[]{:S(2)}) collective-permute-start(f32[144,128]{1,0:T(8,128)S(1)} %get-tuple-element.112), channel_id=1, source_target_pairs={{0,1},{1,2},{2,3},{4,5},{5,6},{6,7},{8,9},{9,10},{10,11},{12,13},{... | collective-permute-start | bytes 221192 | tf_op jit(solution)/shard_map/ppermute | solution.py:428
  66.1 3.2 %collective-permute-done.234.right = f32[144,128]{1,0:T(8,128)S(1)} collective-permute-done((f32[144,128]{1,0:T(8,128)S(1)}, f32[144,128]{1,0:T(8,128)S(1)}, u32[]{:S(2)}, u32[]{:S(2)}) %collective-permute-start.234) | collective-permute-done | bytes 73760 | tf_op jit(solution)/shard_map/ppermute | solution.py:428
  69.4 13.9 %sweeps.1 = f32[16,128,128]{2,1,0:T(8,128)} custom-call(s32[4]{0:T(128)S(1)} %copy-done.4, f32[16,128,128]{2,1,0:T(8,128)S(1)} %bitcast.15, f32[16,128,128]{2,1,0:T(8,128)S(1)} %bitcast.18, f32[128,128]{1,0:T(8,128)S(1)} %bitcast.21, s32[128,128]{1,0:T(8,128)S(1)} %copy-done.2, f32[32,8,128]{2,1,0:T(8,128)S(1)} %collective-permute-done.229.top, ...), custom_call_target="tpu_custom_call" | custom-call | tf_op jit(solution)/shard_map/sweeps/pallas_call | solution.py:413
  (18 shorter events, 0.1 us)
Async XLA Ops:
  1.0 19.2 %collective-permute-start.228 = (f32[4,128,128]{2,1,0:T(8,128)S(1)}, f32[4,128,128]{2,1,0:T(8,128)S(1)}, u32[]{:S(2)}, u32[]{:S(2)}) collective-permute-start(f32[4,128,128]{2,1,0:T(8,128)S(1)} %dynamic-slice_bitcast_fusion.surf), channel_id=1, source_target_pairs={{0,64},{4,68},{8,72},{12,76},{16,80},{20,84},{24,88},{28,92},{32,9... | collective-permute-start | bytes 786440 | tf_op jit(solution)/shard_map/ppermute | solution.py:511
  5.4 14.7 %collective-permute-start.229 = (f32[32,8,128]{2,1,0:T(8,128)}, f32[32,8,128]{2,1,0:T(8,128)S(1)}, u32[]{:S(2)}, u32[]{:S(2)}) collective-permute-start(f32[32,8,128]{2,1,0:T(8,128)} %get-tuple-element.100), channel_id=1, source_target_pairs={{0,4},{4,8},{8,12},{12,16},{16,20},{20,24},{24,28},{28,32},{32,36}... | collective-permute-start | bytes 393224 | tf_op jit(solution)/shard_map/ppermute | solution.py:428
  9.2 10.9 %collective-permute-start.230 = (f32[32,8,128]{2,1,0:T(8,128)}, f32[32,8,128]{2,1,0:T(8,128)S(1)}, u32[]{:S(2)}, u32[]{:S(2)}) collective-permute-start(f32[32,8,128]{2,1,0:T(8,128)} %get-tuple-element.101), channel_id=1, source_target_pairs={{4,0},{8,4},{12,8},{16,12},{20,16},{24,20},{28,24},{32,28},{36,32}... | collective-permute-start | bytes 393224 | tf_op jit(solution)/shard_map/ppermute | solution.py:428
  20.2 20.6 %copy-start.2 = (s32[128,128]{1,0:T(8,128)S(1)}, s32[128,128]{1,0:T(8,128)}, u32[]{:S(2)}) copy-start(s32[128,128]{1,0:T(8,128)} %mask.7) | copy-start | bytes 196612
  20.2 20.6 %copy-start.4 = (s32[4]{0:T(128)S(1)}, s32[4]{0:T(128)}, u32[]{:S(2)}) copy-start(s32[4]{0:T(128)} %get-tuple-element.99.par) | copy-start | bytes 52
  20.2 38.7 %copy-start = (f32[1,16,128,128]{3,2,1,0:T(8,128)S(1)}, f32[1,16,128,128]{3,2,1,0:T(8,128)}, u32[]{:S(2)}) copy-start(f32[1,16,128,128]{3,2,1,0:T(8,128)} %param.70) | copy-start | bytes 3145732
  20.2 38.6 %copy-start.1 = (f32[1,16,128,128]{3,2,1,0:T(8,128)S(1)}, f32[1,16,128,128]{3,2,1,0:T(8,128)}, u32[]{:S(2)}) copy-start(f32[1,16,128,128]{3,2,1,0:T(8,128)} %param.72) | copy-start | bytes 3145732
  20.2 38.6 %copy-start.3 = (f32[1,128,128]{2,1,0:T(8,128)S(1)}, f32[1,128,128]{2,1,0:T(8,128)}, u32[]{:S(2)}) copy-start(f32[1,128,128]{2,1,0:T(8,128)} %param.71) | copy-start | bytes 196612
  20.3 20.5 %collective-permute-start.13 = (f32[4,128,128]{2,1,0:T(8,128)S(1)}, f32[4,128,128]{2,1,0:T(8,128)}, u32[]{:S(2)}, u32[]{:S(2)}) collective-permute-start(f32[4,128,128]{2,1,0:T(8,128)S(1)} %param.35), channel_id=1, source_target_pairs={{76,64},{84,68},{92,72},{100,76},{108,80},{116,84},{124,88},{68,92... | collective-permute-start | bytes 786440 | tf_op jit(solution)/shard_map/cond/branch_35_fun/ppermute | solution.py:451
  22.3 18.4 %collective-permute-start.12 = (f32[4,128,128]{2,1,0:T(8,128)S(1)}, f32[4,128,128]{2,1,0:T(8,128)}, u32[]{:S(2)}, u32[]{:S(2)}) collective-permute-start(f32[4,128,128]{2,1,0:T(8,128)S(1)} %param.35), channel_id=1, source_target_pairs={{72,64},{80,68},{88,72},{96,76},{104,80},{112,84},{120,88},{64,92}... | collective-permute-start | bytes 786440 | tf_op jit(solution)/shard_map/cond/branch_35_fun/ppermute | solution.py:451
  25.3 11.3 %collective-permute-start.15 = (f32[4,64,128]{2,1,0:T(8,128)S(1)}, f32[4,64,128]{2,1,0:T(8,128)}, u32[]{:S(2)}, u32[]{:S(2)}) collective-permute-start(f32[4,64,128]{2,1,0:T(8,128)S(1)} %slice.267), channel_id=1, source_target_pairs={{72,64},{80,68},{88,72},{96,76},{104,80},{112,84},{120,88},{64,92}... | collective-permute-start | bytes 393224 | tf_op jit(solution)/shard_map/cond/branch_35_fun/ppermute | solution.py:451
  31.1 9.7 %collective-permute-start.14 = (f32[4,64,128]{2,1,0:T(8,128)S(1)}, f32[4,64,128]{2,1,0:T(8,128)}, u32[]{:S(2)}, u32[]{:S(2)}) collective-permute-start(f32[4,64,128]{2,1,0:T(8,128)S(1)} %slice.267), channel_id=1, source_target_pairs={{68,64},{76,68},{84,72},{92,76},{100,80},{108,84},{116,88},{124,92... | collective-permute-start | bytes 393224 | tf_op jit(solution)/shard_map/cond/branch_35_fun/ppermute | solution.py:451
  42.1 11.0 %collective-permute-start.232 = (f32[8,128]{1,0:T(8,128)S(1)}, f32[8,128]{1,0:T(8,128)S(1)}, u32[]{:S(2)}, u32[]{:S(2)}) collective-permute-start(f32[8,128]{1,0:T(8,128)S(1)} %get-tuple-element.177), channel_id=1, source_target_pairs={{4,0},{8,4},{12,8},{16,12},{20,16},{24,20},{28,24},{32,28},{36,32}... | collective-permute-start | bytes 12296 | tf_op jit(solution)/shard_map/ppermute | solution.py:428
  51.2 7.6 %collective-permute-start.231 = (f32[8,128]{1,0:T(8,128)S(1)}, f32[8,128]{1,0:T(8,128)S(1)}, u32[]{:S(2)}, u32[]{:S(2)}) collective-permute-start(f32[8,128]{1,0:T(8,128)S(1)} %get-tuple-element.178), channel_id=1, source_target_pairs={{0,4},{4,8},{8,12},{12,16},{16,20},{20,24},{24,28},{28,32},{32,36}... | collective-permute-start | bytes 12296 | tf_op jit(solution)/shard_map/ppermute | solution.py:428
  61.8 4.3 %collective-permute-start.233 = (f32[144,128]{1,0:T(8,128)S(1)}, f32[144,128]{1,0:T(8,128)S(1)}, u32[]{:S(2)}, u32[]{:S(2)}) collective-permute-start(f32[144,128]{1,0:T(8,128)S(1)} %get-tuple-element.111), channel_id=1, source_target_pairs={{1,0},{2,1},{3,2},{5,4},{6,5},{7,6},{9,8},{10,9},{11,10},{13,12},{... | collective-permute-start | bytes 221192 | tf_op jit(solution)/shard_map/ppermute | solution.py:428
  63.7 5.7 %collective-permute-start.234 = (f32[144,128]{1,0:T(8,128)S(1)}, f32[144,128]{1,0:T(8,128)S(1)}, u32[]{:S(2)}, u32[]{:S(2)}) collective-permute-start(f32[144,128]{1,0:T(8,128)S(1)} %get-tuple-element.112), channel_id=1, source_target_pairs={{0,1},{1,2},{2,3},{4,5},{5,6},{6,7},{8,9},{9,10},{10,11},{12,13},{... | collective-permute-start | bytes 221192 | tf_op jit(solution)/shard_map/ppermute | solution.py:428

commit v3 on v2

v3 whole, which is shorter than its diff:
```python
import functools

import jax
import jax.numpy as jnp
from jax import lax
from jax.experimental import pallas as pl
from jax.experimental.pallas import tpu as pltpu
from jax.sharding import PartitionSpec as P

F = 4
SWEEPS = 4
LEV = 16
N = 128
HALO = 8
ROWS = N + 2 * HALO
GX = 16
UNIT = 64

coupling = (0.8, 0.6, 0.4, 0.3)

f32 = jnp.float32
VMEM = pl.BlockSpec(memory_space=pltpu.VMEM)
SMEM = pl.BlockSpec(memory_space=pltpu.SMEM)

PACK = (
    [(4 * q, 4) for q in range(LEV)]
    + [(64 + 3 * i, 3) for i in range(LEV - 1)]
    + [(109, 3), (112, 3)]
)


def params(vmem_mib):
    return pltpu.CompilerParams(vmem_limit_bytes=vmem_mib * 2**20)


CHUNKS = 16


def band_kernel(w_hbm, out_ref, w_ref, sems):
    rows = N // CHUNKS

    def copy(i):
        at = pl.ds(i * rows, rows)
        return pltpu.make_async_copy(w_hbm.at[at], w_ref.at[at], sems.at[i])

    for i in range(CHUNKS):
        copy(i).start()
    sub = lax.broadcasted_iota(jnp.int32, (8, N), 0)
    lane = lax.broadcasted_iota(jnp.int32, (8, N), 1)
    same = sub == lane % 8
    after = sub == (lane + 7) % 8

    def body(i, carry):
        copy(i).wait()
        base = pl.multiple_of(i * rows, rows)
        for k in range(2):
            own, nxt = [], []
            for x in range(rows):
                tile = w_ref[base + x, k, 0:8, :]
                for t in range(1, N // 8):
                    tile = tile + w_ref[base + x, k, 8 * t : 8 * t + 8, :]
                own.append(jnp.sum(jnp.where(same, tile, 0.0), axis=0, keepdims=True))
                nxt.append(jnp.sum(jnp.where(after, tile, 0.0), axis=0, keepdims=True))
            out_ref[k, pl.ds(base, rows)] = jnp.concatenate(own, axis=0)
            out_ref[2 + k, pl.ds(base, rows)] = jnp.concatenate(nxt, axis=0)
        return carry

    lax.fori_loop(0, CHUNKS, body, 0)


def band(weight):
    return pl.pallas_call(
        band_kernel,
        in_specs=[pl.BlockSpec(memory_space=pl.ANY)],
        out_specs=VMEM,
        out_shape=jax.ShapeDtypeStruct((4, N, N), f32),
        scratch_shapes=[pltpu.VMEM((N, 2, N, N), f32), pltpu.SemaphoreType.DMA((CHUNKS,))],
        compiler_params=params(48),
        cost_estimate=pl.CostEstimate(flops=2**22, bytes_accessed=2**24, transcendentals=0),
        name="band",
    )(weight)


def shift_kernel(where, source, par, choice):
    comp, x = where[0], where[1]
    first = source[0, 0]
    units = lax.rem(first // UNIT + 128 - jnp.where(comp == 1, 4, 1) * x, 32)
    par[0] = comp
    par[1] = x
    par[2] = lax.rem(first, UNIT)
    par[3] = units
    choice[0] = comp * 32 + units


def shift(where, source):
    return pl.pallas_call(
        shift_kernel,
        in_specs=[SMEM, SMEM],
        out_specs=[SMEM, SMEM],
        out_shape=[jax.ShapeDtypeStruct((4,), jnp.int32), jax.ShapeDtypeStruct((1,), jnp.int32)],
        name="shift",
    )(where, source)


def force_kernel(
    par, a, b, c1, c2, diag, surf, mask, state, mixing, kappa, out, first, last,
    window, rows, m_ref, k_ref, sems,
):
    comp, x, e, units = par[0], par[1], par[2], par[3]
    copies = []
    for side, (edge, low) in enumerate(((first, 0), (last, N - HALO))):
        at = pl.ds(low, HALO)
        for n, (src, dst) in enumerate(
            (
                (state.at[:, at], edge.at[pl.ds(0, LEV)]),
                (mixing.at[:, at], m_ref.at[side]),
                (kappa.at[at], k_ref.at[side]),
            )
        ):
            copies.append(pltpu.make_async_copy(src, dst, sems.at[3 * side + n]))
    for copy in copies:
        copy.start()

    @pl.when(comp == 1)
    def _():
        odd = units % 2
        low = x < 8
        take_1 = low == (odd == 1)
        base = odd * UNIT
        at_a = pl.multiple_of(jnp.where(low, base, base + N), UNIT)
        at_b = pl.multiple_of(jnp.where(low, base + N, base), UNIT)
        at_c = pl.multiple_of((1 - odd) * 2 * N, UNIT)
        window[:, pl.ds(at_a, N), :] = a[...]
        window[:, pl.ds(at_b, N), :] = b[...]
        window[:, pl.ds(at_c, UNIT), :] = jnp.where(take_1, c1[...], c2[...])
        for f in range(F):
            for k in range(2):
                rows[k, f] = window[f, pl.ds(e + k, N, stride=2), :]

    @pl.when(comp == 0)
    def _():
        odd = (x + units) % 2

        @pl.when(odd == 0)
        def _():
            window[:, 0:N, :] = a[...]

        @pl.when(odd == 1)
        def _():
            window[:, 0:UNIT, :] = c1[...]
            window[:, UNIT:N, :] = c2[...]

        for f in range(F):
            for k in range(2):
                half = window[f, pl.ds(e + k, UNIT), :]
                rows[k, f, pl.ds(0, UNIT, stride=2), :] = half
                rows[k, f, pl.ds(1, UNIT, stride=2), :] = half

    total = jnp.zeros((N, N), f32)
    for i in range(F):
        scale = jnp.where(comp == 1, coupling[F - 1 - i], coupling[i])
        r0 = rows[0, i]
        r1 = rows[1, i]
        after = diag[2] * r0 + diag[3] * r1
        value = diag[0] * r0 + diag[1] * r1 + pltpu.roll(after, N - 1, 1)
        total = total + scale * jnp.tanh(value)
    own = surf[jnp.where(comp == 1, 0, F - 1)]
    sea = jnp.where(comp == 1, mask[...].astype(f32), 1.0)
    forcing = (total - own) * sea
    out[...] = forcing
    for copy in copies:
        copy.wait()
    for side, (edge, low) in enumerate(((first, 0), (last, N - HALO))):
        land_free = sea[low : low + HALO]
        for level in range(LEV - 1):
            edge[LEV + level] = m_ref[side, level] * land_free
        edge[2 * LEV - 1] = k_ref[side] * land_free
        edge[2 * LEV] = forcing[low : low + HALO]


def force(par, pieces, diag, surf, mask, *fields):
    edge = jax.ShapeDtypeStruct((2 * LEV + 1, HALO, N), f32)
    return pl.pallas_call(
        force_kernel,
        in_specs=[SMEM] + [VMEM] * 7 + [pl.BlockSpec(memory_space=pl.ANY)] * 3,
        out_specs=[VMEM, VMEM, VMEM],
        out_shape=[jax.ShapeDtypeStruct((N, N), f32), edge, edge],
        scratch_shapes=[
            pltpu.VMEM((F, 5 * UNIT + 8, N), f32),
            pltpu.VMEM((2, F, N, N), f32),
            pltpu.VMEM((2, LEV, HALO, N), f32),
            pltpu.VMEM((2, HALO, N), f32),
            pltpu.SemaphoreType.DMA((6,)),
        ],
        compiler_params=params(16),
        name="force",
    )(par, *pieces, diag, surf, mask, *fields)


def packed(get):
    lane = lax.broadcasted_iota(jnp.int32, (8, N), 1)
    first = jnp.zeros((8, N), f32)
    last = jnp.zeros((8, N), f32)
    for q, (at, width) in enumerate(PACK):
        value = get(q)
        place = (lane >= at) & (lane < at + width)
        first = jnp.where(place, pltpu.roll(value, at, 1), first)
        last = jnp.where(place, pltpu.roll(value, (at + width) % N, 1), last)
    return first, last


def column_kernel(par, state, mixing, kappa, mask, forcing, left, right, sea):
    ocean = par[0] == 1
    sea[...] = jnp.where(ocean, mask[...].astype(f32), 1.0)

    def body(t, carry):
        rows = pl.ds(pl.multiple_of(t * 8, 8), 8)
        s = sea[rows]

        def get(q):
            if q < LEV:
                return state[q, rows]
            if q < 2 * LEV - 1:
                return mixing[q - LEV, rows] * s
            if q < 2 * LEV:
                return kappa[rows] * s
            return forcing[rows]

        out = pl.ds(pl.multiple_of(HALO + t * 8, 8), 8)
        left[out], right[out] = packed(get)
        return carry

    lax.fori_loop(0, N // 8, body, 0)


def columns(par, *arrays):
    shape = jax.ShapeDtypeStruct((ROWS, N), f32)
    return pl.pallas_call(
        column_kernel,
        in_specs=[SMEM] + [VMEM] * 5,
        out_specs=[VMEM, VMEM],
        out_shape=[shape, shape],
        scratch_shapes=[pltpu.VMEM((N, N), f32)],
        compiler_params=params(16),
        cost_estimate=pl.CostEstimate(flops=2**23, bytes_accessed=2**22, transcendentals=0),
        name="columns",
    )(par, *arrays)


def corner_kernel(top, bottom, left_in, right_in, left, right):
    middle = slice(HALO, HALO + N)
    left[middle] = left_in[middle]
    right[middle] = right_in[middle]
    for halo, rows in ((top, slice(0, HALO)), (bottom, slice(HALO + N, ROWS))):
        left[rows], right[rows] = packed(lambda q, halo=halo: halo[q])


def corners(*arrays):
    shape = jax.ShapeDtypeStruct((ROWS, N), f32)
    return pl.pallas_call(
        corner_kernel,
        in_specs=[VMEM] * 4,
        out_specs=[VMEM, VMEM],
        out_shape=[shape, shape],
        compiler_params=params(16),
        name="corners",
    )(*arrays)


PAD = ROWS + 16
GROUP = 6
BLOCKS = ROWS // (8 * GROUP)
FIELDS = 2 * LEV + 1
KAP = 2 * LEV - 1
FRC = 2 * LEV
SETS = 4
SET = 32
TILES = 6
STRIP = 8 * TILES


def factors(nu, shape):
    before = ratio = None
    for level in range(LEV):
        pivot = jnp.ones(shape, f32)
        if level > 0:
            pivot = pivot + before
        if level < LEV - 1:
            here = nu(level)
            pivot = pivot + here
        if level > 0:
            pivot = pivot - before * ratio
        inverse = 1.0 / pivot
        low = before * inverse if level > 0 else None
        if level < LEV - 1:
            ratio = here * inverse
            before = here
        yield level, inverse, low, ratio if level < LEV - 1 else None


def sweep(ocean, u, at, inv, below, above, kap, frc, rows, store):
    tiles = range(len(at))
    kappa = [kap[r] for r in rows]
    keep = [1.0 - 4.0 * x for x in kappa]
    top_force = jnp.where(ocean, 1.0, 0.0)
    bottom_force = jnp.where(ocean, 0.0, 1.0)
    part = []
    for level in range(LEV):
        row = []
        for i in tiles:
            c = u[level, pl.ds(pl.multiple_of(at[i], 8), 8)]
            up = u[level, pl.ds(at[i] - 1, 8)]
            down = u[level, pl.ds(at[i] + 1, 8)]
            sides = pltpu.roll(c, 1, 1) + pltpu.roll(c, N - 1, 1)
            rhs = keep[i] * c + kappa[i] * ((up + down) + sides)
            if level == 0:
                rhs = rhs + top_force * frc[rows[i]]
            if level == LEV - 1:
                rhs = rhs + bottom_force * frc[rows[i]]
            value = rhs * inv[level, rows[i]]
            if level > 0:
                value = value + below[level, rows[i]] * part[-1][i]
            row.append(value)
        part.append(row)
    v = part[LEV - 1]
    for level in range(LEV - 1, -1, -1):
        if level < LEV - 1:
            v = [part[level][i] + above[level, rows[i]] * v[i] for i in tiles]
        for i in tiles:
            store(level, i, v[i])


def clear_ends(u, rows):
    zero = jnp.zeros((8, N), f32)
    for level in range(LEV):
        u[level, 0:8] = zero
        u[level, rows - 8 : rows] = zero


def aligned(at):
    return pl.ds(pl.multiple_of(at, 8), 8)


def inner_kernel(
    par, state, mixing, kappa, mask, top, bottom, forcing, out, strips,
    u0, ua, ub, nu, inv, below, above, kap, frc,
):
    ocean = par[0] == 1
    for u in (u0, ua, ub):
        clear_ends(u, PAD)

    def tiles(getters, rows):
        for get, at in zip(getters, rows):
            for level in range(LEV):
                u0[level, aligned(at + 8)] = get(level)
            kap[aligned(at)] = get(KAP)
            frc[aligned(at)] = get(FRC)
        steps = [factors(lambda level, get=get: get(LEV + level), (8, N)) for get in getters]
        for level in range(LEV):
            for get, at, step in zip(getters, rows, steps):
                _, inverse, low, high = next(step)
                inv[level, aligned(at)] = inverse
                if low is not None:
                    below[level, aligned(at)] = low
                if high is not None:
                    above[level, aligned(at)] = high
                    nu[level, aligned(at)] = get(LEV + level)

    tiles([lambda q: top[q], lambda q: bottom[q]], [0, HALO + N])

    def body(t, carry):
        getters, rows = [], []
        for i in range(4):
            src = aligned(t * 32 + 8 * i)
            sea = jnp.where(ocean, mask[src].astype(f32), 1.0)

            def get(q, src=src, sea=sea):
                if q < LEV:
                    return state[q, src]
                if q < KAP:
                    return mixing[q - LEV, src] * sea
                if q < FRC:
                    return kappa[src] * sea
                return forcing[src]

            getters.append(get)
            rows.append(t * 32 + 8 * i + HALO)
        tiles(getters, rows)
        return carry

    lax.fori_loop(0, N // 32, body, 0)

    lane = lax.broadcasted_iota(jnp.int32, (8, N), 1)

    def strip(j, carry):
        here = aligned(8 * j)
        for q in range(FIELDS):
            value = jnp.zeros((8, N), f32)
            for g in range(SETS):
                rows = aligned(8 * j + SET * g)
                if q < LEV:
                    c = u0[q, aligned(8 * j + SET * g + 8)]
                elif q < KAP:
                    c = nu[q - LEV, rows]
                else:
                    c = kap[rows] if q == KAP else frc[rows]
                first = SET * g
                high = (lane >= first) & (lane < first + 8)
                low = (lane >= first + 16) & (lane < first + 24)
                value = jnp.where(high, pltpu.roll(c, (first + 8) % N, 1), value)
                value = jnp.where(low, pltpu.roll(c, first + 16, 1), value)
            strips[q, here] = value
        return carry

    lax.fori_loop(0, TILES, strip, 0)

    for s in range(SWEEPS - 1):
        u, u_next = ((u0, ua), (ua, ub), (ub, ua))[s]

        def body(b, carry, u=u, u_next=u_next):
            rows = [aligned(8 * GROUP * b + 8 * i) for i in range(GROUP)]
            at = [8 * GROUP * b + 8 * i + 8 for i in range(GROUP)]

            def store(level, i, v):
                u_next[level, aligned(at[i])] = v

            sweep(ocean, u, at, inv, below, above, kap, frc, rows, store)
            return carry

        lax.fori_loop(0, BLOCKS, body, 0)

    def last(b, carry):
        base = 32 * b
        rows = [aligned(base + HALO + 8 * i) for i in range(4)]
        at = [base + HALO + 8 * i + 8 for i in range(4)]

        def store(level, i, v):
            out[level, aligned(base + 8 * i)] = v

        sweep(ocean, ua, at, inv, below, above, kap, frc, rows, store)
        return carry

    lax.fori_loop(0, N // 32, last, 0)


def inner(par, *arrays):
    wide = pltpu.VMEM((LEV, PAD, N), f32)
    rows = pltpu.VMEM((LEV, ROWS, N), f32)
    flat = pltpu.VMEM((ROWS, N), f32)
    return pl.pallas_call(
        inner_kernel,
        in_specs=[SMEM] + [VMEM] * 7,
        out_specs=[VMEM] * 2,
        out_shape=[
            jax.ShapeDtypeStruct((LEV, N, N), f32),
            jax.ShapeDtypeStruct((FIELDS, STRIP, N), f32),
        ],
        scratch_shapes=[wide] * 3 + [rows] * 4 + [flat] * 2,
        compiler_params=params(32),
        cost_estimate=pl.CostEstimate(flops=2**25, bytes_accessed=2**23, transcendentals=0),
        name="inner",
    )(par, *arrays)


def outer_kernel(
    par, inside, strips, left, right, out, sa, sb, nu, inv, below, above, kap, frc
):
    ocean = par[0] == 1
    lane = lax.broadcasted_iota(jnp.int32, (8, N), 1)
    for u in (sa, sb):
        clear_ends(u, STRIP + 16)

    def build(j, carry):
        here = aligned(8 * j)
        after, before = {}, {}
        for g in range(SETS):
            rows = aligned(8 * j + SET * g)
            after[g] = left[rows]
            before[g] = {4: pltpu.roll(right[rows], 4, 1), 3: pltpu.roll(right[rows], 5, 1)}
        for q, (at, width) in enumerate(PACK):
            value = strips[q, here]
            for g in range(SETS):
                both = jnp.where(
                    (lane >= at) & (lane < at + width),
                    after[g],
                    jnp.where((lane >= at + 8 - width) & (lane < at + 8), before[g][width], 0.0),
                )
                first = SET * g + 8
                place = (lane >= first) & (lane < first + 8)
                value = jnp.where(place, pltpu.roll(both, (first - at) % N, 1), value)
            if q < LEV:
                sa[q, aligned(8 * j + 8)] = value
            elif q < KAP:
                nu[q - LEV, here] = value
            elif q == KAP:
                kap[here] = value
            else:
                frc[here] = value
        return carry

    lax.fori_loop(0, TILES, build, 0)
    for level, inverse, low, high in factors(lambda level: nu[level], (STRIP, N)):
        inv[level] = inverse
        if low is not None:
            below[level] = low
        if high is not None:
            above[level] = high

    def pair(s, carry):
        for u, u_next in ((sa, sb), (sb, sa)):

            def store(level, i, v, u_next=u_next):
                u_next[level, 8 * i + 8 : 8 * i + 16] = v

            sweep(
                ocean, u, [8 * i + 8 for i in range(TILES)], inv, below, above, kap, frc,
                [slice(8 * i, 8 * i + 8) for i in range(TILES)], store,
            )
        return carry

    lax.fori_loop(0, SWEEPS // 2, pair, 0)

    def merge(level, carry):
        for m in range(N // 8):
            g, j = m // 4, m % 4 + 1
            edge = sa[level, 8 * j + 8 : 8 * j + 16]
            value = inside[level, 8 * m : 8 * m + 8]
            value = jnp.where(lane < 4, pltpu.roll(edge, (N - SET * g - 16) % N, 1), value)
            value = jnp.where(lane >= N - 4, pltpu.roll(edge, (N - SET * g - 8) % N, 1), value)
            out[level, 8 * m : 8 * m + 8] = value
        return carry

    lax.fori_loop(0, LEV, merge, 0)


def outer(par, *arrays):
    strip = pltpu.VMEM((LEV, STRIP + 16, N), f32)
    rows = pltpu.VMEM((LEV, STRIP, N), f32)
    flat = pltpu.VMEM((STRIP, N), f32)
    return pl.pallas_call(
        outer_kernel,
        in_specs=[SMEM] + [VMEM] * 4,
        out_specs=VMEM,
        out_shape=jax.ShapeDtypeStruct((LEV, N, N), f32),
        scratch_shapes=[strip] * 2 + [rows] * 4 + [flat] * 2,
        compiler_params=params(24),
        name="outer",
    )(par, *arrays)


def shift_pair(low_edge, high_edge, axis):
    count = lax.axis_size(axis)
    up = [(i, i + 1) for i in range(count - 1)]
    down = [(i + 1, i) for i in range(count - 1)]
    return lax.ppermute(high_edge, axis, up), lax.ppermute(low_edge, axis, down)


BOTH = ("comp", "gx")


MERGED = 16


def ocean_pairs(route):
    return [
        (GX + (2 * x + route % GX + ((x >= 8) != (route >= GX))) % GX, GX + x) for x in range(GX)
    ]


def atmosphere_pairs(route):
    return [((x + route) // 2 % GX, x) for x in range(GX) if (x + route) % 2 == 0]


def listed(block, entry):
    pairs = ocean_pairs((entry + 15) % 32) + atmosphere_pairs(entry)
    if entry == MERGED + 15:
        pairs += atmosphere_pairs(MERGED)
    return lax.ppermute(block, BOTH, pairs)


def atmosphere_routed(block, route):
    route = route % 32
    return listed(block, route if route != MERGED else MERGED + 15)


def ocean_route(units):
    base = units // 2
    odd = units % 2

    def run(peer):
        whole = (base + odd) % GX
        part = (base + 1 - odd) % GX
        half = peer[:, UNIT:] if odd else peer[:, :UNIT]
        jobs = [(peer, whole), (peer, GX + whole), (half, part), (half, GX + part)]
        entries = [(route + 17) % 32 for _, route in jobs]
        if MERGED not in entries:
            return tuple(listed(block, entry) for (block, _), entry in zip(jobs, entries))
        results = []
        last = peer[:1, :8]

        def chained(block, entry):
            nonlocal last
            block, _ = lax.optimization_barrier((block, last))
            last = listed(block, entry)
            return last

        for (block, _), entry in zip(jobs, entries):
            if entry != MERGED:
                results.append(chained(block, entry))
            else:
                low, high = chained(block, 17), chained(block, 31)
                results.append(jnp.where(lax.axis_index("gx") < 8, low, high))
        return tuple(results)

    return run


def atmosphere_route(units):
    def run(peer):
        return (
            atmosphere_routed(peer, units),
            peer,
            atmosphere_routed(peer[:, UNIT:], units - 1),
            atmosphere_routed(peer[:, :UNIT], units + 1),
        )

    return run


def shards(state, diffusivity, mixing, sea_mask, source_row, regrid_weight):
    comp = lax.axis_index("comp")
    gx = lax.axis_index("gx")
    field = state[0]
    mix = mixing[0]
    kappa = diffusivity[0]
    surf = lax.dynamic_slice(field, ((LEV - F) * (1 - comp), 0, 0), (F, N, N))
    swap = [(x, GX + x) for x in range(GX)] + [(GX + x, x) for x in range(GX)]
    peer = lax.ppermute(surf, BOTH, swap)
    where = jnp.stack([comp, gx]).astype(jnp.int32)
    source = jnp.transpose(source_row[0, :, 0, :])
    par, choice = shift(where, source)
    diag = band(regrid_weight[0])
    peer, diag = lax.optimization_barrier((peer, diag))
    pieces = lax.switch(
        choice[0],
        [atmosphere_route(i) for i in range(32)] + [ocean_route(i) for i in range(32)],
        peer,
    )
    forcing, low, high = force(par, pieces, diag, surf, sea_mask, field, mix, kappa)
    top, bottom = shift_pair(low, high, "gx")
    first, last = columns(par, field, mix, kappa, sea_mask, forcing)
    first, last = corners(top, bottom, first, last)
    before, after = shift_pair(first, last, "gy")
    inside, strips = inner(par, field, mix, kappa, sea_mask, top, bottom, forcing)
    return outer(par, inside, strips, after, before)[None]


def solution(mesh):
    placed = (
        P("comp", None, "gx", "gy"),
        P("comp", "gx", "gy"),
        P("comp", None, "gx", "gy"),
        P("gx", "gy"),
        P("comp", "gx", "gy", None),
        P("comp", "gx", None, "gy", None),
    )
    return jax.shard_map(
        shards, mesh=mesh, in_specs=placed, out_specs=P("comp", None, "gx", "gy"), check_vma=False
    )
```

time: 82.9 us -> 70.3 us (0.85)
  the two profiles are of different devices: /device:TPU:30 before, /device:TPU:113 now
where the time goes in v3:
time: 70.3 us; the launch traced here: 70.5 us
  starting transfers between devices  33.5 us (48%)
  Pallas kernels  25.6 us (36%)
  waiting for transfers between devices  8.88 us (13%)
  local copies, waits for them, and re-layouts  1 us (1%)
  between operations  0.8 us (1%)
    ppermute x4, starting transfers between devices, listed(): return lax.ppermute(block, BOTH, pairs)  15.7 us
    ppermute x2, starting transfers between devices, shift_pair(): lax.ppermute(high_edge, axis, up)  13.4 us
    pallas_call x1, Pallas kernels, inner(): pl.pallas_call(inner_kernel, in_specs=[SMEM] + [VMEM] * 7, out_specs=[VME...  7.59 us
    pallas_call x1, Pallas kernels, outer(): pl.pallas_call(outer_kernel, in_specs=[SMEM] + [VMEM] * 4, out_specs=VMEM...  6.32 us
    pallas_call x1, Pallas kernels, band(): pl.pallas_call(band_kernel, in_specs=[pl.BlockSpec(memory_space=pl.ANY)],...  6.01 us
    ppermute x2, waiting for transfers between devices, shift_pair(): lax.ppermute(low_edge, axis, down)  4.89 us
    ppermute x2, starting transfers between devices, shift_pair(): lax.ppermute(low_edge, axis, down)  4.24 us
    ppermute x4, waiting for transfers between devices, listed(): return lax.ppermute(block, BOTH, pairs)  3.88 us
  transfers between devices with their start and end apart: 9, of which 4 were waited for; matrix products, arithmetic and copies ran while one was open for 1% of the time, Pallas kernels for 25%

profile of v3, /device:TPU:113, one launch (start us, length us, event | category | flops | bytes accessed | tf_op | source)
XLA Modules:
  0.0 70.5 jit_solution(14338999826318693872)
XLA Ops:
  0.0 1.0 %dynamic-slice_bitcast_fusion.surf = f32[4,128,128]{2,1,0:T(8,128)S(1)} fusion(f32[1,16,128,128]{3,2,1,0:T(8,128)} %param.70, s32[]{:T(128)S(6)} %select_n.31), kind=kLoop, calls=%fused_computation.4 | loop fusion | bytes 524292 | tf_op jit(solution)/shard_map/dynamic_slice | solution.py:636
  1.0 0.1 collective-permute-start.228
  1.1 0.6 pad_add_fusion.where
  1.7 1.2 %shift.1 = (s32[4]{0:T(128)}, s32[1]{0:T(128)}) custom-call(s32[2]{0:T(128)} %pad_add_fusion.where, s32[2,128]{1,0:T(2,128)} %bitcast.23), custom_call_target="tpu_custom_call" | custom-call | tf_op jit(solution)/shard_map/shift/pallas_call | solution.py:96
  3.6 6.0 %band.1.diag = f32[4,128,128]{2,1,0:T(8,128)S(1)} custom-call(f32[128,2,128,128]{3,2,1,0:T(8,128)} %bitcast.22), custom_call_target="tpu_custom_call" | custom-call | flops 4194304 | bytes 16777216 | tf_op jit(solution)/shard_map/band/pallas_call | solution.py:72
  9.6 0.1 collective-permute-done.228
  9.8 19.7 %conditional.1 = (f32[4,128,128]{2,1,0:T(8,128)}, f32[4,128,128]{2,1,0:T(8,128)}, f32[4,64,128]{2,1,0:T(8,128)}, f32[4,64,128]{2,1,0:T(8,128)}) conditional(s32[]{:T(128)} %bitcast.7, f32[4,128,128]{2,1,0:T(8,128)S(1)} %collective-permute-done.228, f32[4,128,128]{2,1,0:T(8,128)S(1)} %collective-permute-done.228, ...), branch_computations={%region_0.0_spmd, %region_1.0_spmd, %region_2.0_spmd, %region_3.0_... | conditional | flops 65540 | bytes 5243154 | solution.py:644
  9.8 4.8 %collective-permute-start.9 = (f32[4,128,128]{2,1,0:T(8,128)S(1)}, f32[4,128,128]{2,1,0:T(8,128)}, u32[]{:S(2)}, u32[]{:S(2)}) collective-permute-start(f32[4,128,128]{2,1,0:T(8,128)S(1)} %param.34), channel_id=1, source_target_pairs={{72,64},{80,68},{88,72},{96,76},{104,80},{112,84},{120,88},{64,92}... | collective-permute-start | bytes 786440 | tf_op jit(solution)/shard_map/cond/branch_34_fun/ppermute | solution.py:578
  14.6 1.9 %collective-permute-start.8 = (f32[4,128,128]{2,1,0:T(8,128)S(1)}, f32[4,128,128]{2,1,0:T(8,128)}, u32[]{:S(2)}, u32[]{:S(2)}) collective-permute-start(f32[4,128,128]{2,1,0:T(8,128)S(1)} %param.34), channel_id=1, source_target_pairs={{68,64},{76,68},{84,72},{92,76},{100,80},{108,84},{116,88},{124,92... | collective-permute-start | bytes 786440 | tf_op jit(solution)/shard_map/cond/branch_34_fun/ppermute | solution.py:578
  16.5 3.5 %collective-permute-start.11 = (f32[4,64,128]{2,1,0:T(8,128)S(1)}, f32[4,64,128]{2,1,0:T(8,128)}, u32[]{:S(2)}, u32[]{:S(2)}) collective-permute-start(f32[4,64,128]{2,1,0:T(8,128)S(1)} %slice.262), channel_id=1, source_target_pairs={{76,64},{84,68},{92,72},{100,76},{108,80},{116,84},{124,88},{68,92... | collective-permute-start | bytes 393224 | tf_op jit(solution)/shard_map/cond/branch_34_fun/ppermute | solution.py:578
  20.0 5.5 %collective-permute-start.10 = (f32[4,64,128]{2,1,0:T(8,128)S(1)}, f32[4,64,128]{2,1,0:T(8,128)}, u32[]{:S(2)}, u32[]{:S(2)}) collective-permute-start(f32[4,64,128]{2,1,0:T(8,128)S(1)} %slice.262), channel_id=1, source_target_pairs={{72,64},{80,68},{88,72},{96,76},{104,80},{112,84},{120,88},{64,92}... | collective-permute-start | bytes 393224 | tf_op jit(solution)/shard_map/cond/branch_34_fun/ppermute | solution.py:578
  25.6 2.2 %collective-permute-done.11 = f32[4,64,128]{2,1,0:T(8,128)} collective-permute-done((f32[4,64,128]{2,1,0:T(8,128)S(1)}, f32[4,64,128]{2,1,0:T(8,128)}, u32[]{:S(2)}, u32[]{:S(2)}) %collective-permute-start.11) | collective-permute-done | bytes 131104 | tf_op jit(solution)/shard_map/cond/branch_34_fun/ppermute | solution.py:578
  27.8 1.7 %collective-permute-done.10 = f32[4,64,128]{2,1,0:T(8,128)} collective-permute-done((f32[4,64,128]{2,1,0:T(8,128)S(1)}, f32[4,64,128]{2,1,0:T(8,128)}, u32[]{:S(2)}, u32[]{:S(2)}) %collective-permute-start.10) | collective-permute-done | bytes 131104 | tf_op jit(solution)/shard_map/cond/branch_34_fun/ppermute | solution.py:578
  29.5 1.5 %force.1 = (f32[128,128]{1,0:T(8,128)S(1)}, f32[33,8,128]{2,1,0:T(8,128)S(1)}, f32[33,8,128]{2,1,0:T(8,128)S(1)}) custom-call(s32[4]{0:T(128)S(1)} %copy-done.4, f32[4,128,128]{2,1,0:T(8,128)} %get-tuple-element.105.a, f32[4,128,128]{2,1,0:T(8,128)} %get-tuple-element.106.b, f32[4,64,128]{2,1,0:T(8,128)} %get-tuple-element.107.c1, ...), custom_call_target="tpu_custom_call" | custom-call | tf_op jit(solution)/shard_map/force/pallas_call | solution.py:183
  31.0 8.9 %collective-permute-start.229 = (f32[33,8,128]{2,1,0:T(8,128)S(1)}, f32[33,8,128]{2,1,0:T(8,128)S(1)}, u32[]{:S(2)}, u32[]{:S(2)}) collective-permute-start(f32[33,8,128]{2,1,0:T(8,128)S(1)} %get-tuple-element.110), channel_id=1, source_target_pairs={{0,4},{4,8},{8,12},{12,16},{16,20},{20,24},{24,28},{28,32},{32,36}... | collective-permute-start | bytes 405512 | tf_op jit(solution)/shard_map/ppermute | solution.py:555
  39.9 1.9 %collective-permute-start.230 = (f32[33,8,128]{2,1,0:T(8,128)S(1)}, f32[33,8,128]{2,1,0:T(8,128)S(1)}, u32[]{:S(2)}, u32[]{:S(2)}) collective-permute-start(f32[33,8,128]{2,1,0:T(8,128)S(1)} %get-tuple-element.111), channel_id=1, source_target_pairs={{4,0},{8,4},{12,8},{16,12},{20,16},{24,20},{28,24},{32,28},{36,32}... | collective-permute-start | bytes 405512 | tf_op jit(solution)/shard_map/ppermute | solution.py:555
  41.9 2.8 %columns.1 = (f32[144,128]{1,0:T(8,128)S(1)}, f32[144,128]{1,0:T(8,128)S(1)}) custom-call(s32[4]{0:T(128)S(1)} %copy-done.4, f32[16,128,128]{2,1,0:T(8,128)S(1)} %bitcast.14, f32[16,128,128]{2,1,0:T(8,128)S(1)} %bitcast.17, f32[128,128]{1,0:T(8,128)S(1)} %bitcast.20, s32[128,128]{1,0:T(8,128)S(1)} %copy-done.3, f32[128,128]{1,0:T(8,128)S(1)} %get-tuple-element.112.forcing), custom_call_target="tpu_custom_call" | custom-call | flops 8388608 | bytes 4194304 | tf_op jit(solution)/shard_map/columns/pallas_call | solution.py:238
  44.6 0.0 collective-permute-done.229.top
  44.6 4.9 %collective-permute-done.230.bottom = f32[33,8,128]{2,1,0:T(8,128)S(1)} collective-permute-done((f32[33,8,128]{2,1,0:T(8,128)S(1)}, f32[33,8,128]{2,1,0:T(8,128)S(1)}, u32[]{:S(2)}, u32[]{:S(2)}) %collective-permute-start.230) | collective-permute-done | bytes 135200 | tf_op jit(solution)/shard_map/ppermute | solution.py:555
  49.5 0.2 corners.1
  49.7 2.3 %collective-permute-start.231 = (f32[144,128]{1,0:T(8,128)S(1)}, f32[144,128]{1,0:T(8,128)S(1)}, u32[]{:S(2)}, u32[]{:S(2)}) collective-permute-start(f32[144,128]{1,0:T(8,128)S(1)} %get-tuple-element.117), channel_id=1, source_target_pairs={{1,0},{2,1},{3,2},{5,4},{6,5},{7,6},{9,8},{10,9},{11,10},{13,12},{... | collective-permute-start | bytes 221192 | tf_op jit(solution)/shard_map/ppermute | solution.py:555
  52.0 4.5 %collective-permute-start.232 = (f32[144,128]{1,0:T(8,128)S(1)}, f32[144,128]{1,0:T(8,128)S(1)}, u32[]{:S(2)}, u32[]{:S(2)}) collective-permute-start(f32[144,128]{1,0:T(8,128)S(1)} %get-tuple-element.118), channel_id=1, source_target_pairs={{0,1},{1,2},{2,3},{4,5},{5,6},{6,7},{8,9},{9,10},{10,11},{12,13},{... | collective-permute-start | bytes 221192 | tf_op jit(solution)/shard_map/ppermute | solution.py:555
  56.6 7.6 %inner.1 = (f32[16,128,128]{2,1,0:T(8,128)S(1)}, f32[33,48,128]{2,1,0:T(8,128)S(1)}) custom-call(s32[4]{0:T(128)S(1)} %copy-done.4, f32[16,128,128]{2,1,0:T(8,128)S(1)} %bitcast.15, f32[16,128,128]{2,1,0:T(8,128)S(1)} %bitcast.18, f32[128,128]{1,0:T(8,128)S(1)} %bitcast.21, s32[128,128]{1,0:T(8,128)S(1)} %copy-done.3, ...), custom_call_target="tpu_custom_call" | custom-call | flops 33554432 | bytes 8388608 | tf_op jit(solution)/shard_map/inner/pallas_call | solution.py:450
  64.2 6.3 %outer.1 = f32[16,128,128]{2,1,0:T(8,128)} custom-call(s32[4]{0:T(128)S(1)} %copy-done.4, f32[16,128,128]{2,1,0:T(8,128)S(1)} %get-tuple-element.113.inside, f32[33,48,128]{2,1,0:T(8,128)S(1)} %get-tuple-element.114.strips, f32[144,128]{1,0:T(8,128)S(1)} %collective-permute-done.231.left, f32[144,128]{1,0:T(8,128)S(1)} %collective-permute-done.232.right), custom_call_target="tpu_custom_call" | custom-call | tf_op jit(solution)/shard_map/outer/pallas_call | solution.py:540
  (15 shorter events, 0.0 us)
Async XLA Ops:
  1.0 8.8 %collective-permute-start.228 = (f32[4,128,128]{2,1,0:T(8,128)S(1)}, f32[4,128,128]{2,1,0:T(8,128)S(1)}, u32[]{:S(2)}, u32[]{:S(2)}) collective-permute-start(f32[4,128,128]{2,1,0:T(8,128)S(1)} %dynamic-slice_bitcast_fusion.surf), channel_id=1, source_target_pairs={{0,64},{4,68},{8,72},{12,76},{16,80},{20,84},{24,88},{28,92},{32,9... | collective-permute-start | bytes 786440 | tf_op jit(solution)/shard_map/ppermute | solution.py:638
  9.7 19.7 %copy-start = (f32[1,16,128,128]{3,2,1,0:T(8,128)S(1)}, f32[1,16,128,128]{3,2,1,0:T(8,128)}, u32[]{:S(2)}) copy-start(f32[1,16,128,128]{3,2,1,0:T(8,128)} %param.70) | copy-start | bytes 3145732
  9.7 19.7 %copy-start.1 = (f32[1,16,128,128]{3,2,1,0:T(8,128)S(1)}, f32[1,16,128,128]{3,2,1,0:T(8,128)}, u32[]{:S(2)}) copy-start(f32[1,16,128,128]{3,2,1,0:T(8,128)} %param.72) | copy-start | bytes 3145732
  9.7 19.7 %copy-start.2 = (f32[1,128,128]{2,1,0:T(8,128)S(1)}, f32[1,128,128]{2,1,0:T(8,128)}, u32[]{:S(2)}) copy-start(f32[1,128,128]{2,1,0:T(8,128)} %param.71) | copy-start | bytes 196612
  9.7 19.8 %copy-start.3 = (s32[128,128]{1,0:T(8,128)S(1)}, s32[128,128]{1,0:T(8,128)}, u32[]{:S(2)}) copy-start(s32[128,128]{1,0:T(8,128)} %mask.5) | copy-start | bytes 196612
  9.7 19.8 %copy-start.4 = (s32[4]{0:T(128)S(1)}, s32[4]{0:T(128)}, u32[]{:S(2)}) copy-start(s32[4]{0:T(128)} %get-tuple-element.102.par) | copy-start | bytes 52
  9.8 19.6 %collective-permute-start.9 = (f32[4,128,128]{2,1,0:T(8,128)S(1)}, f32[4,128,128]{2,1,0:T(8,128)}, u32[]{:S(2)}, u32[]{:S(2)}) collective-permute-start(f32[4,128,128]{2,1,0:T(8,128)S(1)} %param.34), channel_id=1, source_target_pairs={{72,64},{80,68},{88,72},{96,76},{104,80},{112,84},{120,88},{64,92}... | collective-permute-start | bytes 786440 | tf_op jit(solution)/shard_map/cond/branch_34_fun/ppermute | solution.py:578
  14.6 14.9 %collective-permute-start.8 = (f32[4,128,128]{2,1,0:T(8,128)S(1)}, f32[4,128,128]{2,1,0:T(8,128)}, u32[]{:S(2)}, u32[]{:S(2)}) collective-permute-start(f32[4,128,128]{2,1,0:T(8,128)S(1)} %param.34), channel_id=1, source_target_pairs={{68,64},{76,68},{84,72},{92,76},{100,80},{108,84},{116,88},{124,92... | collective-permute-start | bytes 786440 | tf_op jit(solution)/shard_map/cond/branch_34_fun/ppermute | solution.py:578
  16.5 11.3 %collective-permute-start.11 = (f32[4,64,128]{2,1,0:T(8,128)S(1)}, f32[4,64,128]{2,1,0:T(8,128)}, u32[]{:S(2)}, u32[]{:S(2)}) collective-permute-start(f32[4,64,128]{2,1,0:T(8,128)S(1)} %slice.262), channel_id=1, source_target_pairs={{76,64},{84,68},{92,72},{100,76},{108,80},{116,84},{124,88},{68,92... | collective-permute-start | bytes 393224 | tf_op jit(solution)/shard_map/cond/branch_34_fun/ppermute | solution.py:578
  20.0 9.4 %collective-permute-start.10 = (f32[4,64,128]{2,1,0:T(8,128)S(1)}, f32[4,64,128]{2,1,0:T(8,128)}, u32[]{:S(2)}, u32[]{:S(2)}) collective-permute-start(f32[4,64,128]{2,1,0:T(8,128)S(1)} %slice.262), channel_id=1, source_target_pairs={{72,64},{80,68},{88,72},{96,76},{104,80},{112,84},{120,88},{64,92}... | collective-permute-start | bytes 393224 | tf_op jit(solution)/shard_map/cond/branch_34_fun/ppermute | solution.py:578
  31.0 13.6 %collective-permute-start.229 = (f32[33,8,128]{2,1,0:T(8,128)S(1)}, f32[33,8,128]{2,1,0:T(8,128)S(1)}, u32[]{:S(2)}, u32[]{:S(2)}) collective-permute-start(f32[33,8,128]{2,1,0:T(8,128)S(1)} %get-tuple-element.110), channel_id=1, source_target_pairs={{0,4},{4,8},{8,12},{12,16},{16,20},{20,24},{24,28},{28,32},{32,36}... | collective-permute-start | bytes 405512 | tf_op jit(solution)/shard_map/ppermute | solution.py:555
  39.9 9.6 %collective-permute-start.230 = (f32[33,8,128]{2,1,0:T(8,128)S(1)}, f32[33,8,128]{2,1,0:T(8,128)S(1)}, u32[]{:S(2)}, u32[]{:S(2)}) collective-permute-start(f32[33,8,128]{2,1,0:T(8,128)S(1)} %get-tuple-element.111), channel_id=1, source_target_pairs={{4,0},{8,4},{12,8},{16,12},{20,16},{24,20},{28,24},{32,28},{36,32}... | collective-permute-start | bytes 405512 | tf_op jit(solution)/shard_map/ppermute | solution.py:555
  49.7 14.4 %collective-permute-start.231 = (f32[144,128]{1,0:T(8,128)S(1)}, f32[144,128]{1,0:T(8,128)S(1)}, u32[]{:S(2)}, u32[]{:S(2)}) collective-permute-start(f32[144,128]{1,0:T(8,128)S(1)} %get-tuple-element.117), channel_id=1, source_target_pairs={{1,0},{2,1},{3,2},{5,4},{6,5},{7,6},{9,8},{10,9},{11,10},{13,12},{... | collective-permute-start | bytes 221192 | tf_op jit(solution)/shard_map/ppermute | solution.py:555
  52.0 12.1 %collective-permute-start.232 = (f32[144,128]{1,0:T(8,128)S(1)}, f32[144,128]{1,0:T(8,128)S(1)}, u32[]{:S(2)}, u32[]{:S(2)}) collective-permute-start(f32[144,128]{1,0:T(8,128)S(1)} %get-tuple-element.118), channel_id=1, source_target_pairs={{0,1},{1,2},{2,3},{4,5},{5,6},{6,7},{8,9},{9,10},{10,11},{12,13},{... | collective-permute-start | bytes 221192 | tf_op jit(solution)/shard_map/ppermute | solution.py:555
